TPU v7x, 512 devices: a whole 4x4x16 slice. The times are simulated.
512 devices in a mesh: tm: 16 (over z), space: 32 (over y, x, core).
Axes of the slice: x: 4, y: 4, z: 16, core: 2. Of those that a mesh axis runs over, the one named last changes fastest.
Arguments:
- c_points: float32 [16, 5, 2048, 512], P('tm', None, 'space'), may hold values from -6 to 6
- terminal: float32 [5, 2048, 512], P(None, 'space'), may hold values from -6 to 6
- forcing: bfloat16 [16, 4, 5, 2048, 512], P('tm', None, None, 'space'), may hold values from -4 to 4
- conductance: float32 [2048, 512], P('space'), may hold values from 0.05 to 0.25
- coupling: float32 [5, 5], replicated
- flap_cells: int32 [1024, 128], P('space'), may hold values from -1 to 32767, as said below
- flap_actuator: int32 [1024, 128], P('space'), may hold values from -1 to 3, as said below
- flap_area: float32 [1024, 128], P('space'), may hold values from 0.5 to 2
- actuator_rate: float32 [128], P('space'), may hold values from 0.0046875 to 0.046875
Outputs:
- new_points: float32 [16, 5, 2048, 512], P('tm', None, 'space')
- actuator_adjoint: float32 [16, 4, 128], P('tm', None, 'space')
Inputs may be any that keep to these rules, and one draw needn't show every extreme that they name: `flap_cells`: empty slots hold -1; every live slot names a cell of the sending device's block. One owner gets 128 live slots from every device; other devices may send nothing. Each device's full tile names its last cell in some slot. `flap_actuator`: -1 exactly where flap_cells is -1, else an actuator of the owner.
All inputs are finite; a program needn't handle non-finite values.
Results may differ from a plain program's by a relative error of at most 0.00105.
Values may be sent and summed in bfloat16 or wider, within the bound.
A program may use at most 64 MiB of HBM per device.

v0:
```python
import jax
import jax.numpy as jnp
from jax import lax
from jax.sharding import PartitionSpec as P

STEPS = 4
ACT_DEV = 4


def shifted(block, axis, distance):
    devices = range(lax.axis_size(axis))
    route = [(i - distance, i) for i in devices if i - distance in devices]
    return lax.ppermute(block, axis, route)


def with_halo(block, sides, width):
    for axis, dim in sides:
        count = lax.axis_size(axis)
        forward = [(i, i + 1) for i in range(count - 1)]
        backward = [(target, source) for source, target in forward]
        low = lax.ppermute(
            lax.slice_in_dim(block, block.shape[dim] - width, None, axis=dim), axis, forward
        )
        high = lax.ppermute(lax.slice_in_dim(block, 0, width, axis=dim), axis, backward)
        block = jnp.concatenate([low, block, high], axis=dim)
    return block


def entering(value, axis, join, neutral):
    count, mine = (lax.axis_size(axis), lax.axis_index(axis))
    pieces = jax.tree.map(lambda part: lax.all_gather(part, axis), value)
    pieces = jax.tree.map(lambda part: part[::-1], pieces)
    mine = count - 1 - mine
    total = jax.tree.map(
        lambda part, zero: jnp.full_like(part, 0) + jnp.asarray(zero, part.dtype), value, neutral
    )

    def step(position, total):
        longer = join(total, jax.tree.map(lambda part: part[position], pieces))
        return jax.tree.map(lambda new, old: jnp.where(position < mine, new, old), longer, total)

    return lax.fori_loop(0, count - 1, step, total)


def stencil(padded, center, conductance, coupling):
    padded = jnp.pad(padded, ((0, 0), (0, 0), (1, 1)))
    north = padded[:, :-2, 1:-1]
    south = padded[:, 2:, 1:-1]
    west = padded[:, 1:-1, :-2]
    east = padded[:, 1:-1, 2:]
    beside = 0.35 * north + 0.15 * south + 0.3 * west + 0.2 * east
    mixed = center + conductance * (beside - center)
    return jnp.einsum("gf,grc->frc", coupling, mixed, precision=lax.Precision.HIGHEST)


def face_values(lam, flap_cells, flap_area):
    energy = lam[4].reshape(-1)
    live = flap_cells >= 0
    picked = energy[jnp.maximum(flap_cells, 0)]
    return jnp.where(live, picked * flap_area, 0.0)


def relax(lam, forcing_steps, conductance, coupling, flap_cells, flap_area, extend):
    faces = [None] * STEPS
    for step in reversed(range(STEPS)):
        lam = stencil(extend(lam), lam, conductance, coupling)
        lam = lam + forcing_steps[step].astype(jnp.float32)
        faces[step] = face_values(lam, flap_cells, flap_area)
    return (lam, jnp.stack(faces, axis=1))


def chain_combine(earlier, later):
    return (earlier[0] * later[0], later[0] * earlier[1] + later[1])


def per_device(
    c_points,
    terminal,
    forcing,
    conductance,
    coupling,
    flap_cells,
    flap_actuator,
    flap_area,
    actuator_rate,
):
    own_points = c_points[0]
    arrived = shifted(own_points, "tm", -1)
    is_last = lax.axis_index("tm") == lax.axis_size("tm") - 1
    start = arrived + jnp.where(is_last, terminal, 0.0)

    def extend(field):
        return with_halo(field.astype(jnp.bfloat16), (("space", 1),), 1).astype(field.dtype)

    lam, faces = relax(start, forcing[0], conductance, coupling, flap_cells, flap_area, extend)
    actuator_ids = jnp.arange(ACT_DEV, dtype=jnp.int32)
    got_values = lax.all_to_all(faces, "space", split_axis=0, concat_axis=0, tiled=True)
    got_ids = lax.all_to_all(flap_actuator, "space", split_axis=0, concat_axis=0, tiled=True)
    onehot = (got_ids[:, :, None] == actuator_ids[None, None, :]).astype(jnp.float32)
    loads = jnp.einsum("skj,sja->ka", got_values, onehot, precision=lax.Precision.HIGHEST)
    decay = jnp.exp(-actuator_rate)
    offset = jnp.zeros_like(decay)
    for step in range(STEPS):
        offset = offset + decay**step * loads[step]
    whole = decay**STEPS
    _, incoming = entering(
        (whole, offset), "tm", chain_combine, (jnp.ones_like(decay), jnp.zeros_like(decay))
    )
    states = [None] * STEPS
    current = incoming
    for step in reversed(range(STEPS)):
        current = decay * current + loads[step]
        states[step] = current
    return (lam[None], jnp.stack(states)[None])


def solution(mesh):
    placed = (
        P("tm", None, "space", None),
        P(None, "space", None),
        P("tm", None, None, "space", None),
        P("space", None),
        P(),
        P("space", None),
        P("space", None),
        P("space", None),
        P("space"),
    )
    return jax.shard_map(
        per_device,
        mesh=mesh,
        in_specs=placed,
        out_specs=(P("tm", None, "space", None), P("tm", None, "space")),
        check_vma=False,
    )
```

profile of v0, /device:TPU:8, one launch (start us, length us, event | category | flops | bytes accessed | tf_op | source)
XLA Modules:
  0.0 215.3 jit_solution(16705484019576682679)
XLA Ops:
  0.6 0.0 copy-start
  0.6 0.0 copy-start.1
  0.7 1.4 collective-permute-start
  2.1 17.5 %collective-permute-done = f32[5,64,512]{2,1,0:T(8,128)S(1)} collective-permute-done((f32[5,64,512]{2,1,0:T(8,128)}, f32[5,64,512]{2,1,0:T(8,128)S(1)}, u32[]{:S(2)}, u32[]{:S(2)}) %collective-permute-start) | collective-permute-done | bytes 655392 | tf_op jit(solution)/shard_map/ppermute | solution.py:13
  19.5 1.9 fusion.48
  21.4 1.9 collective-permute-start.1
  23.3 5.8 %collective-permute-start.2 = (bf16[5,1,512]{2,0,1:T(8,128)(2,1)S(1)}, bf16[5,1,512]{2,0,1:T(8,128)(2,1)S(1)}, u32[]{:S(2)}, u32[]{:S(2)}) collective-permute-start(bf16[5,1,512]{2,0,1:T(8,128)(2,1)S(1)} %get-tuple-element.148), channel_id=1, source_target_pairs={{1,0},{2,1},{3,2},{4,3},{5,4},{6,5},{7,6},{8,7},{9,8},{10,9},{11,1... | collective-permute-start | bytes 15368 | tf_op jit(solution)/shard_map/ppermute | solution.py:24
  29.1 0.0 copy-done.1
  29.1 0.1 fusion.108
  29.2 0.0 copy-start.2
  29.3 0.0 copy-start.7
  29.3 0.0 collective-permute-done.1
  29.3 1.2 collective-permute-done.2
  30.5 0.2 maximum_convert_fusion
  30.6 0.0 copy-done
  30.6 0.0 copy-done.2
  30.6 0.0 copy-done.7
  30.6 2.4 %fusion.113 = (bf16[5,64,512]{2,0,1:T(8,128)(2,1)S(1)}, f32[5,64,512]{2,0,1:T(8,128)S(1)}) fusion(bf16[1,1,5,64,512]{4,3,2,1,0:T(8,128)(2,1)S(1)} %get-tuple-element.140, f32[5,5]{1,0:T(8,128)S(1)} %copy-done, f32[5,66,512]{2,0,1:T(8,128)S(1)} %maximum_convert_fusion, f32[5,64,512]{2,1,0:T(8,128)S(1)} %copy-done.2, ...), kind=kOutput, calls=%fused_computation.158 | convolution fusion | flops 12288000 | bytes 5935105 | tf_op jit(solution)/shard_map/gf,grc->frc/dot_general | solution.py:53
  33.1 0.0 copy-start.5
  33.1 1.9 collective-permute-start.3
  35.0 5.8 %collective-permute-start.4 = (bf16[5,1,512]{2,0,1:T(8,128)(2,1)S(1)}, bf16[5,1,512]{2,0,1:T(8,128)(2,1)S(1)}, u32[]{:S(2)}, u32[]{:S(2)}) collective-permute-start(bf16[5,1,512]{2,0,1:T(8,128)(2,1)S(1)} %get-tuple-element.146), channel_id=1, source_target_pairs={{1,0},{2,1},{3,2},{4,3},{5,4},{6,5},{7,6},{8,7},{9,8},{10,9},{11,1... | collective-permute-start | bytes 15368 | tf_op jit(solution)/shard_map/ppermute | solution.py:24
  40.8 0.0 collective-permute-done.3
  40.8 1.3 collective-permute-done.4
  42.1 0.2 maximum_convert_fusion.1
  42.3 1.9 fusion.114
  44.2 0.0 copy-done.5
  44.2 1.9 collective-permute-start.5
  46.1 5.8 %collective-permute-start.6 = (bf16[5,1,512]{2,0,1:T(8,128)(2,1)S(1)}, bf16[5,1,512]{2,0,1:T(8,128)(2,1)S(1)}, u32[]{:S(2)}, u32[]{:S(2)}) collective-permute-start(bf16[5,1,512]{2,0,1:T(8,128)(2,1)S(1)} %get-tuple-element.144), channel_id=1, source_target_pairs={{1,0},{2,1},{3,2},{4,3},{5,4},{6,5},{7,6},{8,7},{9,8},{10,9},{11,1... | collective-permute-start | bytes 15368 | tf_op jit(solution)/shard_map/ppermute | solution.py:24
  51.9 5.1 %all-to-all-start.1 = ((s32[32,1,128]{2,1,0:T(1,128)}), s32[32,1,128]{2,1,0:T(1,128)S(1)}, u32[]{:S(2)}, u32[]{:S(2)}) async-start(s32[32,1,128]{2,1,0:T(1,128)} %bitcast.31), calls=%async_computation.1 | async-start | bytes 32768 | tf_op jit(solution)/shard_map/all_to_all | solution.py:98
  57.0 0.0 collective-permute-done.5
  57.0 0.0 collective-permute-done.6
  57.0 0.2 maximum_convert_fusion.2
  57.2 0.0 copy-start.3
  57.2 1.8 fusion.115
  59.1 2.1 collective-permute-start.7
  61.1 5.8 %collective-permute-start.8 = (bf16[5,1,512]{2,0,1:T(8,128)(2,1)S(1)}, bf16[5,1,512]{2,0,1:T(8,128)(2,1)S(1)}, u32[]{:S(2)}, u32[]{:S(2)}) collective-permute-start(bf16[5,1,512]{2,0,1:T(8,128)(2,1)S(1)} %get-tuple-element.142), channel_id=1, source_target_pairs={{1,0},{2,1},{3,2},{4,3},{5,4},{6,5},{7,6},{8,7},{9,8},{10,9},{11,1... | collective-permute-start | bytes 15368 | tf_op jit(solution)/shard_map/ppermute | solution.py:24
  67.0 1.3 dynamic-slice
  68.9 1.4 slice.187
  70.2 23.0 %gather_fusion.3 = f32[4096]{0:T(1024)S(1)} fusion(f32[32768]{0:T(1024)S(1)} %bitcast.151, s32[4096]{0:T(1024)S(1)} %bitcast_clamp_fusion), kind=kCustom, calls=%fused_computation.3 | custom fusion | bytes 49152 | tf_op jit(solution)/shard_map/gather | solution.py:59
  93.3 0.1 slice.186
  93.4 23.0 %gather_fusion.2 = f32[4096]{0:T(1024)S(1)} fusion(f32[32768]{0:T(1024)S(1)} %bitcast.152, s32[4096]{0:T(1024)S(1)} %bitcast_clamp_fusion), kind=kCustom, calls=%fused_computation.2 | custom fusion | bytes 49152 | tf_op jit(solution)/shard_map/gather | solution.py:59
  116.5 0.1 slice.185
  116.6 23.0 %gather_fusion.1 = f32[4096]{0:T(1024)S(1)} fusion(f32[32768]{0:T(1024)S(1)} %bitcast.154, s32[4096]{0:T(1024)S(1)} %bitcast_clamp_fusion), kind=kCustom, calls=%fused_computation.1 | custom fusion | bytes 49152 | tf_op jit(solution)/shard_map/gather | solution.py:59
  139.7 0.0 collective-permute-done.7
  139.7 0.0 collective-permute-done.8
  139.7 0.2 maximum_convert_fusion.3
  139.8 1.8 fusion
  141.7 0.1 slice.184
  141.8 0.0 copy-start.4
  141.8 0.0 copy-start.6
  141.9 23.0 %gather_fusion = f32[4096]{0:T(1024)S(1)} fusion(f32[32768]{0:T(1024)S(1)} %bitcast.153, s32[4096]{0:T(1024)S(1)} %bitcast_clamp_fusion), kind=kCustom, calls=%fused_computation | custom fusion | bytes 49152 | tf_op jit(solution)/shard_map/gather | solution.py:59
  164.9 0.7 pad_maximum_fusion
  165.6 0.0 all-to-all-done.1
  165.6 5.3 %all-to-all-start = ((f32[32,4,128]{2,1,0:T(4,128)}), f32[32,4,128]{2,1,0:T(4,128)S(1)}, u32[]{:S(2)}, u32[]{:S(2)}) async-start(f32[32,4,128]{2,1,0:T(4,128)} %pad_maximum_fusion), calls=%async_computation | async-start | bytes 131072 | tf_op jit(solution)/shard_map/all_to_all | solution.py:97
  170.9 0.1 fusion.85
  171.0 1.2 copy.52
  172.3 5.0 %all-to-all-done = f32[32,4,128]{2,1,0:T(4,128)S(1)} async-done(((f32[32,4,128]{2,1,0:T(4,128)}), f32[32,4,128]{2,1,0:T(4,128)S(1)}, u32[]{:S(2)}, u32[]{:S(2)}) %all-to-all-start) | async-done | bytes 65568 | tf_op jit(solution)/shard_map/all_to_all | solution.py:97
  177.2 0.2 convolution_bitcast_fusion.4
  177.5 0.1 fusion.81
  177.6 36.3 %all-reduce.6 = (f32[64]{0:T(128)S(1)}, f32[64]{0:T(128)S(1)}) all-reduce(f32[64]{0:T(128)S(1)} %fusion.85, f32[64]{0:T(128)S(1)} %fusion.81), channel_id=2, replica_groups=mesh['tm'=16,'space'=32] {'tm'}, use_global_device_ids=true, to_apply=%add.4 | all-reduce | flops 128 | bytes 1024
  213.9 0.1 reshape.61
  214.0 0.1 reshape.62
  214.1 0.6 while.14
  214.7 0.6 maximum_bitcast_fusion
  (32 shorter events, 0.4 us)
Async XLA Ops:
  0.6 30.0 %copy-start = (f32[5,5]{1,0:T(8,128)S(1)}, f32[5,5]{1,0:T(8,128)}, u32[]{:S(2)}) copy-start(f32[5,5]{1,0:T(8,128)} %param.15) | copy-start | bytes 304
  0.6 28.5 %copy-start.1 = (bf16[1,4,5,64,512]{4,3,2,1,0:T(8,128)(2,1)S(1)}, bf16[1,4,5,64,512]{4,3,2,1,0:T(8,128)(2,1)}, u32[]{:S(2)}) copy-start(bf16[1,4,5,64,512]{4,3,2,1,0:T(8,128)(2,1)} %param.13) | copy-start | bytes 3932164
  0.7 18.9 %collective-permute-start = (f32[5,64,512]{2,1,0:T(8,128)}, f32[5,64,512]{2,1,0:T(8,128)S(1)}, u32[]{:S(2)}, u32[]{:S(2)}) collective-permute-start(f32[5,64,512]{2,1,0:T(8,128)} %bitcast.162), channel_id=1, source_target_pairs={{32,0},{64,32},{96,64},{128,96},{160,128},{192,160},{224,192},{256... | collective-permute-start | bytes 1966088 | tf_op jit(solution)/shard_map/ppermute | solution.py:13
  21.4 7.9 %collective-permute-start.1 = (bf16[5,1,512]{2,0,1:T(8,128)(2,1)S(1)}, bf16[5,1,512]{2,0,1:T(8,128)(2,1)S(1)}, u32[]{:S(2)}, u32[]{:S(2)}) collective-permute-start(bf16[5,1,512]{2,0,1:T(8,128)(2,1)S(1)} %get-tuple-element.147), channel_id=1, source_target_pairs={{0,1},{1,2},{2,3},{3,4},{4,5},{5,6},{6,7},{7,8},{8,9},{9,10},{10,1... | collective-permute-start | bytes 15368 | tf_op jit(solution)/shard_map/ppermute | solution.py:21
  23.3 7.1 %collective-permute-start.2 = (bf16[5,1,512]{2,0,1:T(8,128)(2,1)S(1)}, bf16[5,1,512]{2,0,1:T(8,128)(2,1)S(1)}, u32[]{:S(2)}, u32[]{:S(2)}) collective-permute-start(bf16[5,1,512]{2,0,1:T(8,128)(2,1)S(1)} %get-tuple-element.148), channel_id=1, source_target_pairs={{1,0},{2,1},{3,2},{4,3},{5,4},{6,5},{7,6},{8,7},{9,8},{10,9},{11,1... | collective-permute-start | bytes 15368 | tf_op jit(solution)/shard_map/ppermute | solution.py:24
  29.2 1.4 copy-start.2
  29.3 1.4 copy-start.7
  33.1 11.1 %copy-start.5 = (f32[5,64,512]{2,0,1:T(8,128)}, f32[5,64,512]{2,0,1:T(8,128)S(1)}, u32[]{:S(2)}) copy-start(f32[5,64,512]{2,0,1:T(8,128)S(1)} %get-tuple-element.154) | copy-start | bytes 1966084
  33.1 7.7 %collective-permute-start.3 = (bf16[5,1,512]{2,0,1:T(8,128)(2,1)S(1)}, bf16[5,1,512]{2,0,1:T(8,128)(2,1)S(1)}, u32[]{:S(2)}, u32[]{:S(2)}) collective-permute-start(bf16[5,1,512]{2,0,1:T(8,128)(2,1)S(1)} %get-tuple-element.145), channel_id=1, source_target_pairs={{0,1},{1,2},{2,3},{3,4},{4,5},{5,6},{6,7},{7,8},{8,9},{9,10},{10,1... | collective-permute-start | bytes 15368 | tf_op jit(solution)/shard_map/ppermute | solution.py:21
  35.0 7.1 %collective-permute-start.4 = (bf16[5,1,512]{2,0,1:T(8,128)(2,1)S(1)}, bf16[5,1,512]{2,0,1:T(8,128)(2,1)S(1)}, u32[]{:S(2)}, u32[]{:S(2)}) collective-permute-start(bf16[5,1,512]{2,0,1:T(8,128)(2,1)S(1)} %get-tuple-element.146), channel_id=1, source_target_pairs={{1,0},{2,1},{3,2},{4,3},{5,4},{6,5},{7,6},{8,7},{9,8},{10,9},{11,1... | collective-permute-start | bytes 15368 | tf_op jit(solution)/shard_map/ppermute | solution.py:24
  44.2 12.8 %collective-permute-start.5 = (bf16[5,1,512]{2,0,1:T(8,128)(2,1)S(1)}, bf16[5,1,512]{2,0,1:T(8,128)(2,1)S(1)}, u32[]{:S(2)}, u32[]{:S(2)}) collective-permute-start(bf16[5,1,512]{2,0,1:T(8,128)(2,1)S(1)} %get-tuple-element.143), channel_id=1, source_target_pairs={{0,1},{1,2},{2,3},{3,4},{4,5},{5,6},{6,7},{7,8},{8,9},{9,10},{10,1... | collective-permute-start | bytes 15368 | tf_op jit(solution)/shard_map/ppermute | solution.py:21
  46.1 10.9 %collective-permute-start.6 = (bf16[5,1,512]{2,0,1:T(8,128)(2,1)S(1)}, bf16[5,1,512]{2,0,1:T(8,128)(2,1)S(1)}, u32[]{:S(2)}, u32[]{:S(2)}) collective-permute-start(bf16[5,1,512]{2,0,1:T(8,128)(2,1)S(1)} %get-tuple-element.144), channel_id=1, source_target_pairs={{1,0},{2,1},{3,2},{4,3},{5,4},{6,5},{7,6},{8,7},{9,8},{10,9},{11,1... | collective-permute-start | bytes 15368 | tf_op jit(solution)/shard_map/ppermute | solution.py:24
  51.9 113.7 %all-to-all-start.1 = ((s32[32,1,128]{2,1,0:T(1,128)}), s32[32,1,128]{2,1,0:T(1,128)S(1)}, u32[]{:S(2)}, u32[]{:S(2)}) async-start(s32[32,1,128]{2,1,0:T(1,128)} %bitcast.31), calls=%async_computation.1 | async-start | bytes 32768 | tf_op jit(solution)/shard_map/all_to_all | solution.py:98
  57.2 9.7 %copy-start.3 = (s32[32,128]{1,0:T(8,128)S(1)}, s32[32,128]{1,0:T(8,128)}, u32[]{:S(2)}) copy-start(s32[32,128]{1,0:T(8,128)} %param.16) | copy-start | bytes 49156
  59.1 80.6 %collective-permute-start.7 = (bf16[5,1,512]{2,0,1:T(8,128)(2,1)S(1)}, bf16[5,1,512]{2,0,1:T(8,128)(2,1)S(1)}, u32[]{:S(2)}, u32[]{:S(2)}) collective-permute-start(bf16[5,1,512]{2,0,1:T(8,128)(2,1)S(1)} %get-tuple-element.141), channel_id=1, source_target_pairs={{0,1},{1,2},{2,3},{3,4},{4,5},{5,6},{6,7},{7,8},{8,9},{9,10},{10,1... | collective-permute-start | bytes 15368 | tf_op jit(solution)/shard_map/ppermute | solution.py:21
  61.1 78.6 %collective-permute-start.8 = (bf16[5,1,512]{2,0,1:T(8,128)(2,1)S(1)}, bf16[5,1,512]{2,0,1:T(8,128)(2,1)S(1)}, u32[]{:S(2)}, u32[]{:S(2)}) collective-permute-start(bf16[5,1,512]{2,0,1:T(8,128)(2,1)S(1)} %get-tuple-element.142), channel_id=1, source_target_pairs={{1,0},{2,1},{3,2},{4,3},{5,4},{6,5},{7,6},{8,7},{9,8},{10,9},{11,1... | collective-permute-start | bytes 15368 | tf_op jit(solution)/shard_map/ppermute | solution.py:24
  141.8 23.1 %copy-start.4 = (f32[32,128]{1,0:T(8,128)S(1)}, f32[32,128]{1,0:T(8,128)}, u32[]{:S(2)}) copy-start(f32[32,128]{1,0:T(8,128)} %param.18) | copy-start | bytes 49156
  141.8 29.1 %copy-start.6 = (f32[4]{0:T(128)S(1)}, f32[4]{0:T(128)}, u32[]{:S(2)}) copy-start(f32[4]{0:T(128)} %param.19) | copy-start | bytes 52
  165.6 11.6 %all-to-all-start = ((f32[32,4,128]{2,1,0:T(4,128)}), f32[32,4,128]{2,1,0:T(4,128)S(1)}, u32[]{:S(2)}, u32[]{:S(2)}) async-start(f32[32,4,128]{2,1,0:T(4,128)} %pad_maximum_fusion), calls=%async_computation | async-start | bytes 131072 | tf_op jit(solution)/shard_map/all_to_all | solution.py:97
where the time goes:
time: 216 us; the launch traced here: 215 us
  local copies, waits for them, and re-layouts  96.8 us (45%)
  starting transfers between devices  42.7 us (20%)
  blocking collectives  36.3 us (17%)
  waiting for transfers between devices  24.9 us (12%)
  matrix products  8.21 us (4%)
  other arithmetic  4.34 us (2%)
    gather x4, local copies, waits for them, and re-layouts, face_values(): picked = energy[jnp.maximum(flap_cells, 0)]  92.1 us
    unnamed x1, blocking collectives  36.3 us
    ppermute x4, starting transfers between devices, with_halo(): lax.ppermute(lax.slice_in_dim(block, 0, width, axis=dim), axis, backward)  23.1 us
    ppermute x1, waiting for transfers between devices, shifted(): return lax.ppermute(block, axis, route)  17.5 us
    dot_general x4, matrix products, stencil(): jnp.einsum('gf,grc->frc', coupling, mixed, precision=lax.Precision.HIGHEST)  7.98 us
    ppermute x4, starting transfers between devices, with_halo(): lax.ppermute(lax.slice_in_dim(block, block.shape[dim] - width, None, axis...  7.82 us
    all_to_all x1, starting transfers between devices, per_device(): lax.all_to_all(faces, 'space', split_axis=0, concat_axis=0, tiled=True)  5.27 us
    all_to_all x1, starting transfers between devices, per_device(): lax.all_to_all(flap_actuator, 'space', split_axis=0, concat_axis=0, tiled...  5.09 us
  transfers between devices with their start and end apart: 11, of which 4 were waited for; matrix products, arithmetic and copies ran while one was open for 47% of the time, Pallas kernels for 0%

commit v1 on v0

v1 whole, which is shorter than its diff:
```python
import jax
import jax.numpy as jnp
from jax import lax
from jax.experimental import pallas as pl
from jax.experimental.pallas import tpu as pltpu
from jax.sharding import PartitionSpec as P

STEPS = 4
ACT = 4
FIELDS = 5
ROWS = 64
COLS = 512
LANES = 128
BLOCKS = COLS // LANES
CHUNK = 16
CHUNKS = ROWS // CHUNK
EXT = ROWS + 2 * CHUNK
MESH = pl.DeviceIdType.MESH
LEVELS = 32767.0


def quantize(src, rows_at, dst, scales):
    for piece in range(CHUNKS):
        tile = []
        for f in range(FIELDS):
            x = src[f, pl.ds(piece * CHUNK, CHUNK), :]
            top = jnp.max(jnp.abs(x), axis=(0, 1), keepdims=True)
            safe = jnp.maximum(top, 1e-30)
            y = jnp.round(x * (LEVELS / safe))
            dst[f, pl.ds(rows_at + piece * CHUNK, CHUNK), :] = y.astype(jnp.int32).astype(jnp.int16)
            tile.append(jnp.broadcast_to(safe * (1.0 / LEVELS), (1, LANES)))
        tile += [jnp.zeros((1, LANES), jnp.float32)] * (8 - FIELDS)
        scales[piece] = jnp.concatenate(tile, axis=0)


def exchange(
    points, terminal, forcing, conductance,
    start, scale, force_halo, cond_halo,
    raw, coded, coded_scale, end_scale,
    raw_sem, z_send, z_recv, s_send, s_recv,
):
    nt, ns = lax.axis_size("tm"), lax.axis_size("space")
    t, s = lax.axis_index("tm"), lax.axis_index("space")
    barrier = pltpu.get_barrier_semaphore()
    for dev in (
        (lax.rem(t + nt - 1, nt), s), (lax.rem(t + 1, nt), s),
        (t, lax.rem(s + ns - 1, ns)), (t, lax.rem(s + 1, ns)),
    ):
        pl.semaphore_signal(barrier, inc=1, device_id=dev, device_id_type=MESH)
    load = pltpu.make_async_copy(points.at[0], raw, raw_sem)
    load.start()
    load.wait()
    quantize(raw, 0, coded, coded_scale)
    pl.semaphore_wait(barrier, 4)

    def z_copy(src, dst, i):
        return pltpu.make_async_remote_copy(
            src_ref=src, dst_ref=dst, send_sem=z_send.at[i], recv_sem=z_recv.at[i],
            device_id=(t - 1, s), device_id_type=MESH,
        )

    z_copies = [z_copy(coded_scale, scale.at[pl.ds(1, CHUNKS)], CHUNKS)] + [
        z_copy(
            coded.at[:, pl.ds(p * CHUNK, CHUNK), :],
            start.at[:, pl.ds((p + 1) * CHUNK, CHUNK), :], p,
        )
        for p in (CHUNKS - 1, 0, 1, 2)
    ]

    def s_copy(src, dst, i, to):
        return pltpu.make_async_remote_copy(
            src_ref=src, dst_ref=dst, send_sem=s_send.at[i], recv_sem=s_recv.at[i],
            device_id=(t, to), device_id_type=MESH,
        )

    up_first = [
        s_copy(conductance.at[pl.ds(ROWS - 8, 8)], cond_halo.at[0], 0, s + 1),
        s_copy(
            forcing.at[0, pl.ds(1, 3), :, pl.ds(ROWS - CHUNK, CHUNK), :], force_halo.at[0], 1, s + 1
        ),
    ]
    down_first = [
        s_copy(conductance.at[pl.ds(0, 8)], cond_halo.at[1], 4, s - 1),
        s_copy(forcing.at[0, pl.ds(1, 3), :, pl.ds(0, CHUNK), :], force_halo.at[1], 5, s - 1),
    ]
    up_then = [
        s_copy(scale.at[CHUNKS], scale.at[0], 2, s + 1),
        s_copy(
            start.at[:, pl.ds(ROWS, CHUNK), :], start.at[:, pl.ds(0, CHUNK), :], 3, s + 1
        ),
    ]
    down_then = [
        s_copy(scale.at[1], scale.at[CHUNKS + 1], 6, s - 1),
        s_copy(
            start.at[:, pl.ds(CHUNK, CHUNK), :],
            start.at[:, pl.ds(ROWS + CHUNK, CHUNK), :], 7, s - 1,
        ),
    ]
    has_up, has_down = s < ns - 1, s > 0

    @pl.when(t > 0)
    def _():
        for copy in z_copies:
            copy.start()

    @pl.when(has_up)
    def _():
        for copy in up_first:
            copy.start()

    @pl.when(has_down)
    def _():
        for copy in down_first:
            copy.start()

    @pl.when(t == nt - 1)
    def _():
        end = pltpu.make_async_copy(terminal, raw, raw_sem)
        end.start()
        end.wait()
        quantize(raw, CHUNK, start, end_scale)
        for p in range(CHUNKS):
            scale[p + 1] = end_scale[p]

    @pl.when(t < nt - 1)
    def _():
        for copy in z_copies[:2]:
            copy.wait_recv()

    @pl.when(has_up)
    def _():
        for copy in up_then:
            copy.start()

    @pl.when(t < nt - 1)
    def _():
        z_copies[2].wait_recv()

    @pl.when(has_down)
    def _():
        for copy in down_then:
            copy.start()

    @pl.when(jnp.logical_not(has_down))
    def _():
        cond_halo[0] = jnp.zeros((8, COLS), jnp.float32)
        force_halo[0] = jnp.zeros((3, FIELDS, CHUNK, COLS), jnp.bfloat16)
        scale[0] = jnp.zeros((8, LANES), jnp.float32)
        start[:, pl.ds(0, CHUNK), :] = jnp.zeros((FIELDS, CHUNK, COLS), jnp.int16)

    @pl.when(jnp.logical_not(has_up))
    def _():
        cond_halo[1] = jnp.zeros((8, COLS), jnp.float32)
        force_halo[1] = jnp.zeros((3, FIELDS, CHUNK, COLS), jnp.bfloat16)
        scale[CHUNKS + 1] = jnp.zeros((8, LANES), jnp.float32)
        start[:, pl.ds(ROWS + CHUNK, CHUNK), :] = jnp.zeros((FIELDS, CHUNK, COLS), jnp.int16)

    @pl.when(t < nt - 1)
    def _():
        for copy in z_copies[3:]:
            copy.wait_recv()

    @pl.when(has_down)
    def _():
        for copy in up_first + up_then:
            copy.wait_recv()
        for copy in down_first + down_then:
            copy.wait_send()

    @pl.when(has_up)
    def _():
        for copy in down_first + down_then:
            copy.wait_recv()
        for copy in up_first + up_then:
            copy.wait_send()

    @pl.when(t > 0)
    def _():
        for copy in z_copies:
            copy.wait_send()


def one_tile(src, cond, row, coupling, lane):
    first, last = lane == 0, lane == LANES - 1
    weight = [cond[b, pl.ds(row, 8), :] for b in range(BLOCKS)]
    mixed = []
    for f in range(FIELDS):
        mid = [src[f, b, pl.ds(row, 8), :] for b in range(BLOCKS)]
        left = [pltpu.roll(v, 1, 1) for v in mid]
        right = [pltpu.roll(v, LANES - 1, 1) for v in mid]
        out = []
        for b in range(BLOCKS):
            west = jnp.where(first, left[b - 1] if b else 0.0, left[b])
            east = jnp.where(last, right[b + 1] if b < BLOCKS - 1 else 0.0, right[b])
            north = src[f, b, pl.ds(row - 1, 8), :]
            south = src[f, b, pl.ds(row + 1, 8), :]
            beside = 0.35 * north + 0.15 * south + 0.3 * west + 0.2 * east
            out.append(mid[b] + weight[b] * (beside - mid[b]))
        mixed.append(out)
    result = []
    for f in range(FIELDS):
        row_out = []
        for b in range(BLOCKS):
            total = coupling[0][f] * mixed[0][b]
            for g in range(1, FIELDS):
                total = total + coupling[g][f] * mixed[g][b]
            row_out.append(total)
        result.append(row_out)
    return result


def relax(
    start, scale, forcing, force_halo, conductance, cond_halo, coupling_ref, cells, acts, area,
    points, partial,
    lam_a, lam_b, cond, picked,
):
    lane = lax.broadcasted_iota(jnp.int32, (8, LANES), 1)
    coupling = [[coupling_ref[g, f] for f in range(FIELDS)] for g in range(FIELDS)]

    for b in range(BLOCKS):
        cols = pl.ds(b * LANES, LANES)
        cond[b, pl.ds(8, 8), :] = cond_halo[0, :, cols]
        cond[b, pl.ds(CHUNK, ROWS), :] = conductance[:, cols]
        cond[b, pl.ds(CHUNK + ROWS, 8), :] = cond_halo[1, :, cols]
        for piece in range(CHUNKS + 2):
            rows = pl.ds(piece * CHUNK, CHUNK)
            for f in range(FIELDS):
                factor = scale[piece, f : f + 1, :]
                lam_a[f, b, rows, :] = start[f, rows, cols].astype(jnp.int32).astype(jnp.float32) * factor

    key = lax.shift_right_arithmetic(cells[...], 7)
    slot_lane = jnp.bitwise_and(cells[...], LANES - 1)

    def pick(k, src):
        def body(r, acc):
            for b in range(BLOCKS):
                row = jnp.broadcast_to(src[4, b, pl.ds(CHUNK + r, 1), :], key.shape)
                got = jnp.take_along_axis(row, slot_lane, axis=1, mode="promise_in_bounds")
                acc = jnp.where(key == r * BLOCKS + b, got, acc)
            return acc

        acc = lax.fori_loop(0, ROWS, body, jnp.zeros(key.shape, jnp.float32), unroll=4)
        picked[k] = acc * area[...]

    src, dst = lam_a, lam_b
    for k in reversed(range(STEPS)):
        if k:
            for edge, row in ((0, 8), (1, CHUNK + ROWS)):
                got = one_tile(src, cond, row, coupling, lane)
                for f in range(FIELDS):
                    for b in range(BLOCKS):
                        push = force_halo[edge, k - 1, f, :, pl.ds(b * LANES, LANES)].astype(jnp.float32)
                        push = push[8:] if edge == 0 else push[:8]
                        dst[f, b, pl.ds(row, 8), :] = got[f][b] + push

        def body(j, carry, k=k, src=src, dst=dst):
            for half in range(2):
                at = pl.multiple_of(j * CHUNK, CHUNK)
                row = pl.multiple_of(j * CHUNK + CHUNK + 8 * half, 8)
                got = one_tile(src, cond, row, coupling, lane)
                for f in range(FIELDS):
                    for b in range(BLOCKS):
                        cols = pl.ds(b * LANES, LANES)
                        push = forcing[0, k, f, pl.ds(at, CHUNK), cols].astype(jnp.float32)
                        value = got[f][b] + push[8 * half : 8 * half + 8]
                        if k == 0:
                            points[0, f, pl.ds(at + 8 * half, 8), cols] = value
                        if k or f == 4:
                            dst[f, b, pl.ds(row, 8), :] = value
            return carry

        lax.fori_loop(0, CHUNKS, body, 0)
        pick(k, dst)
        src, dst = dst, src

    ids = acts[...]
    wide = lax.broadcasted_iota(jnp.int32, key.shape, 1)
    total = jnp.zeros(key.shape, jnp.float32)
    for k in range(STEPS):
        values = picked[k]
        for a in range(ACT):
            part = jnp.sum(jnp.where(ids == a, values, 0.0), axis=1, keepdims=True)
            total = jnp.where(jnp.bitwise_and(wide, STEPS * ACT - 1) == k * ACT + a, part, total)
    partial[...] = total.reshape(partial.shape)


def collect(partial, rate, states, mine, later, send, s_send, s_recv, t_send, t_recv):
    nt, ns = lax.axis_size("tm"), lax.axis_size("space")
    t, s = lax.axis_index("tm"), lax.axis_index("space")
    later[...] = jnp.zeros(later.shape, jnp.float32)
    barrier = pltpu.get_barrier_semaphore()

    def greet_space(i, carry):
        pl.semaphore_signal(barrier, inc=1, device_id=(t, lax.rem(s + i, ns)), device_id_type=MESH)
        return carry

    def greet_time(i, carry):
        pl.semaphore_signal(barrier, inc=1, device_id=(lax.rem(t + i, nt), s), device_id_type=MESH)
        return carry

    lax.fori_loop(1, ns, greet_space, 0)
    lax.fori_loop(1, nt, greet_time, 0)
    pl.semaphore_wait(barrier, ns - 1 + nt - 1)

    def to_owner(i):
        d = lax.rem(s + i, ns)
        return pltpu.make_async_remote_copy(
            src_ref=partial.at[d], dst_ref=mine.at[s], send_sem=s_send.at[i], recv_sem=s_recv.at[ns - i],
            device_id=(t, d), device_id_type=MESH,
        )

    lax.fori_loop(1, ns, lambda i, c: (to_owner(i).start(), c)[1], 0)
    mine[s] = partial[s]
    r = rate[...]
    lane = lax.broadcasted_iota(jnp.int32, (1, LANES), 1)
    k_of = lax.rem(lane, STEPS * ACT) // ACT
    k_f = k_of.astype(jnp.float32)
    gap = lax.broadcasted_iota(jnp.int32, later.shape, 0) - t - 1
    weight = jnp.where(gap >= 0, jnp.exp(-(STEPS * 1.0) * gap.astype(jnp.float32) * r[None]), 0.0)
    decay = [jnp.exp(-float(m) * r) for m in range(STEPS)]

    def from_slot(i, c):
        d = lax.rem(s + i, ns)
        pltpu.make_async_remote_copy(
            src_ref=partial.at[d], dst_ref=mine.at[d], send_sem=s_send.at[i], recv_sem=s_recv.at[i],
            device_id=(t, d), device_id_type=MESH,
        ).wait_recv()
        return c

    lax.fori_loop(1, ns, from_slot, 0)
    load = jnp.sum(mine[...], axis=0)
    weighted = load * jnp.exp(-k_f * r)
    for shift in (8, 4):
        weighted = weighted + pltpu.roll(weighted, shift, 1)
    send[...] = weighted

    def earlier(i):
        return pltpu.make_async_remote_copy(
            src_ref=send, dst_ref=later.at[t], send_sem=t_send.at[i], recv_sem=t_recv.at[t],
            device_id=(i, s), device_id_type=MESH,
        )

    lax.fori_loop(0, t, lambda i, c: (earlier(i).start(), c)[1], 0)
    base = load
    for m in range(1, STEPS):
        moved = pltpu.roll(load, LANES - ACT * m, 1)
        base = base + jnp.where(k_of + m < STEPS, decay[m] * moved, 0.0)

    def arrived(i, c):
        pltpu.make_async_remote_copy(
            src_ref=send, dst_ref=later.at[i], send_sem=t_send.at[i], recv_sem=t_recv.at[i],
            device_id=(i, s), device_id_type=MESH,
        ).wait_recv()
        return c

    lax.fori_loop(t + 1, nt, arrived, 0)
    incoming = jnp.sum(later[...] * weight, axis=0)
    states[...] = base + jnp.exp(-(STEPS - k_f) * r) * incoming
    lax.fori_loop(0, t, lambda i, c: (earlier(i).wait_send(), c)[1], 0)
    lax.fori_loop(1, ns, lambda i, c: (to_owner(i).wait_send(), c)[1], 0)


def per_device(
    c_points, terminal, forcing, conductance, coupling, flap_cells, flap_actuator, flap_area, actuator_rate
):
    nt, ns = lax.axis_size("tm"), lax.axis_size("space")
    anywhere = pl.BlockSpec(memory_space=pl.ANY)
    vmem = pl.BlockSpec(memory_space=pltpu.VMEM)
    smem = pl.BlockSpec(memory_space=pltpu.SMEM)
    dma = pltpu.SemaphoreType.DMA
    f32 = jnp.float32
    start, scale, force_halo, cond_halo = pl.pallas_call(
        exchange,
        out_shape=(
            jax.ShapeDtypeStruct((FIELDS, EXT, COLS), jnp.int16),
            jax.ShapeDtypeStruct((CHUNKS + 2, 8, LANES), f32),
            jax.ShapeDtypeStruct((2, STEPS - 1, FIELDS, CHUNK, COLS), jnp.bfloat16),
            jax.ShapeDtypeStruct((2, 8, COLS), f32),
        ),
        in_specs=[anywhere] * 4,
        out_specs=(vmem,) * 4,
        scratch_shapes=[
            pltpu.VMEM((FIELDS, ROWS, COLS), f32),
            pltpu.VMEM((FIELDS, ROWS, COLS), jnp.int16),
            pltpu.VMEM((CHUNKS, 8, LANES), f32),
            pltpu.VMEM((CHUNKS, 8, LANES), f32),
            dma,
            dma((CHUNKS + 1,)), dma((CHUNKS + 1,)), dma((8,)), dma((8,)),
        ],
        compiler_params=pltpu.CompilerParams(
            collective_id=0, has_side_effects=True, vmem_limit_bytes=32 * 2**20
        ),
        name="exchange",
    )(c_points, terminal, forcing, conductance)
    points, partial = pl.pallas_call(
        relax,
        out_shape=(
            jax.ShapeDtypeStruct((1, FIELDS, ROWS, COLS), f32),
            jax.ShapeDtypeStruct((ns, 1, LANES), f32),
        ),
        in_specs=[vmem] * 6 + [smem] + [vmem] * 3,
        out_specs=(vmem, vmem),
        scratch_shapes=[
            pltpu.VMEM((FIELDS, BLOCKS, EXT, LANES), f32),
            pltpu.VMEM((FIELDS, BLOCKS, EXT, LANES), f32),
            pltpu.VMEM((BLOCKS, EXT, LANES), f32),
            pltpu.VMEM((STEPS, ns, LANES), f32),
        ],
        compiler_params=pltpu.CompilerParams(vmem_limit_bytes=32 * 2**20),
        name="relax",
    )(start, scale, forcing, force_halo, conductance, cond_halo, coupling, flap_cells, flap_actuator, flap_area)
    rate = jnp.tile(actuator_rate, LANES // ACT)[None]
    states = pl.pallas_call(
        collect,
        out_shape=jax.ShapeDtypeStruct((1, LANES), f32),
        in_specs=[vmem, vmem],
        out_specs=vmem,
        scratch_shapes=[
            pltpu.VMEM((ns, 1, LANES), f32),
            pltpu.VMEM((nt, 1, LANES), f32),
            pltpu.VMEM((1, LANES), f32),
            dma((ns,)), dma((ns,)), dma((nt,)), dma((nt,)),
        ],
        compiler_params=pltpu.CompilerParams(collective_id=1, has_side_effects=True),
        name="collect",
    )(partial, rate)
    return (points, states[0, : STEPS * ACT].reshape(1, STEPS, ACT))


def solution(mesh):
    placed = (
        P("tm", None, "space", None),
        P(None, "space", None),
        P("tm", None, None, "space", None),
        P("space", None),
        P(),
        P("space", None),
        P("space", None),
        P("space", None),
        P("space"),
    )
    return jax.shard_map(
        per_device,
        mesh=mesh,
        in_specs=placed,
        out_specs=(P("tm", None, "space", None), P("tm", None, "space")),
        check_vma=False,
    )
```

time: 216 us -> 70.5 us (0.33)
  the two profiles are of different devices: /device:TPU:8 before, /device:TPU:1 now
where the time goes in v1:
time: 70.5 us; the launch traced here: 70.2 us
  Pallas kernels  62.5 us (89%)
  local copies, waits for them, and re-layouts  6.99 us (10%)
  between operations  0.72 us (1%)
    pallas_call x1, Pallas kernels, per_device(): pl.pallas_call(collect, out_shape=jax.ShapeDtypeStruct((1, LANES), f32),...  23.5 us
    pallas_call x1, Pallas kernels, per_device(): pl.pallas_call(relax, out_shape=(jax.ShapeDtypeStruct((1, FIELDS, ROWS, C...  20.8 us
    pallas_call x1, Pallas kernels, per_device(): pl.pallas_call(exchange, out_shape=(jax.ShapeDtypeStruct((FIELDS, EXT, CO...  18.2 us
    unnamed x22, local copies, waits for them, and re-layouts  5.02 us

profile of v1, /device:TPU:1, one launch (start us, length us, event | category | flops | bytes accessed | tf_op | source)
XLA Modules:
  0.0 70.2 jit_solution(12918703195691675930)
XLA Ops:
  0.6 0.0 copy-start
  0.6 1.3 %copy-done = bf16[1,4,5,64,512]{4,3,2,1,0:T(8,128)(2,1)S(1)} copy-done((bf16[1,4,5,64,512]{4,3,2,1,0:T(8,128)(2,1)S(1)}, bf16[1,4,5,64,512]{4,3,2,1,0:T(8,128)(2,1)}, u32[]{:S(2)}) %copy-start) | copy-done | bytes 1310744
  1.9 0.0 copy-start.2
  2.0 1.1 %copy-done.2 = f32[1,5,64,512]{3,2,1,0:T(8,128)S(1)} copy-done((f32[1,5,64,512]{3,2,1,0:T(8,128)S(1)}, f32[1,5,64,512]{3,2,1,0:T(8,128)}, u32[]{:S(2)}) %copy-start.2) | copy-done | bytes 655384
  3.0 0.0 copy-start.3
  3.0 1.1 %copy-done.3 = f32[5,64,512]{2,1,0:T(8,128)S(1)} copy-done((f32[5,64,512]{2,1,0:T(8,128)S(1)}, f32[5,64,512]{2,1,0:T(8,128)}, u32[]{:S(2)}) %copy-start.3) | copy-done | bytes 655384
  4.1 0.0 copy-start.4
  4.1 0.9 %copy-done.4 = f32[64,512]{1,0:T(8,128)S(1)} copy-done((f32[64,512]{1,0:T(8,128)S(1)}, f32[64,512]{1,0:T(8,128)}, u32[]{:S(2)}) %copy-start.4) | copy-done | bytes 131096
  5.0 0.0 copy-start.1
  5.0 0.0 copy-start.5
  5.0 0.0 copy-start.6
  5.0 0.0 copy-start.7
  5.0 0.0 copy-start.9
  5.1 18.2 %exchange.1 = (s16[5,96,512]{2,1,0:T(8,128)(2,1)S(1)}, f32[6,8,128]{2,1,0:T(8,128)S(1)}, bf16[2,3,5,16,512]{4,3,2,1,0:T(8,128)(2,1)S(1)}, f32[2,8,512]{2,1,0:T(8,128)S(1)}) custom-call(f32[1,5,64,512]{3,2,1,0:T(8,128)S(1)} %copy-done.2, f32[5,64,512]{2,1,0:T(8,128)S(1)} %copy-done.3, bf16[1,4,5,64,512]{4,3,2,1,0:T(8,128)(2,1)S(1)} %copy-done, ...), custom_call_target="tpu_custom_call" | custom-call | tf_op jit(solution)/shard_map/exchange/pallas_call | solution.py:372
  23.2 0.0 copy-start.10
  23.2 0.0 copy-done.1
  23.2 0.0 copy-done.5
  23.3 0.0 copy-done.6
  23.3 0.0 copy-done.7
  23.3 0.0 copy-done.9
  23.3 20.8 %relax.1 = (f32[1,5,64,512]{3,2,1,0:T(8,128)}, f32[32,1,128]{2,1,0:T(1,128)S(1)}) custom-call(s16[5,96,512]{2,1,0:T(8,128)(2,1)S(1)} %get-tuple-element.8.start, f32[6,8,128]{2,1,0:T(8,128)S(1)} %get-tuple-element.9.scale, bf16[1,4,5,64,512]{4,3,2,1,0:T(8,128)(2,1)S(1)} %copy-done.1, bf16[2,3,5,16,512]{4,3,2,1,0:T(8,128)(2,1)S(1)} %get-tuple-element.10.force_halo, ...), custom_call_target="tpu_custom_call" | custom-call | tf_op jit(solution)/shard_map/relax/pallas_call | solution.py:395
  44.1 0.0 copy-start.8
  44.1 0.6 copy-done.8
  44.7 0.0 copy-done.10
  44.7 0.6 broadcast_in_dim_tile.3.rate
  45.4 23.5 %collect.1 = f32[1,128]{1,0:T(1,128)} custom-call(f32[32,1,128]{2,1,0:T(1,128)} %copy-done.8, f32[1,128]{1,0:T(1,128)} %broadcast_in_dim_tile.3.rate), custom_call_target="tpu_custom_call" | custom-call | tf_op jit(solution)/shard_map/collect/pallas_call | solution.py:413
  68.8 0.7 slice_reduce_fusion
  69.5 0.7 reshape_squeeze.3
  (1 shorter events, 0.0 us)
Async XLA Ops:
  0.6 1.3 %copy-start = (bf16[1,4,5,64,512]{4,3,2,1,0:T(8,128)(2,1)S(1)}, bf16[1,4,5,64,512]{4,3,2,1,0:T(8,128)(2,1)}, u32[]{:S(2)}) copy-start(bf16[1,4,5,64,512]{4,3,2,1,0:T(8,128)(2,1)} %forcing.3) | copy-start | bytes 3932164
  1.9 1.1 %copy-start.2 = (f32[1,5,64,512]{3,2,1,0:T(8,128)S(1)}, f32[1,5,64,512]{3,2,1,0:T(8,128)}, u32[]{:S(2)}) copy-start(f32[1,5,64,512]{3,2,1,0:T(8,128)} %points.1) | copy-start | bytes 1966084
  3.0 1.1 %copy-start.3 = (f32[5,64,512]{2,1,0:T(8,128)S(1)}, f32[5,64,512]{2,1,0:T(8,128)}, u32[]{:S(2)}) copy-start(f32[5,64,512]{2,1,0:T(8,128)} %terminal.1) | copy-start | bytes 1966084
  4.1 0.9 %copy-start.4 = (f32[64,512]{1,0:T(8,128)S(1)}, f32[64,512]{1,0:T(8,128)}, u32[]{:S(2)}) copy-start(f32[64,512]{1,0:T(8,128)} %conductance.3) | copy-start | bytes 393220
  5.0 18.2 %copy-start.1 = (bf16[1,4,5,64,512]{4,3,2,1,0:T(8,128)(2,1)S(1)}, bf16[1,4,5,64,512]{4,3,2,1,0:T(8,128)(2,1)}, u32[]{:S(2)}) copy-start(bf16[1,4,5,64,512]{4,3,2,1,0:T(8,128)(2,1)} %forcing.3) | copy-start | bytes 3932164
  5.0 18.2 %copy-start.5 = (s32[32,128]{1,0:T(8,128)S(1)}, s32[32,128]{1,0:T(8,128)}, u32[]{:S(2)}) copy-start(s32[32,128]{1,0:T(8,128)} %cells.1) | copy-start | bytes 49156
  5.0 18.2 %copy-start.6 = (s32[32,128]{1,0:T(8,128)S(1)}, s32[32,128]{1,0:T(8,128)}, u32[]{:S(2)}) copy-start(s32[32,128]{1,0:T(8,128)} %acts.1) | copy-start | bytes 49156
  5.0 18.2 %copy-start.7 = (f32[32,128]{1,0:T(8,128)S(1)}, f32[32,128]{1,0:T(8,128)}, u32[]{:S(2)}) copy-start(f32[32,128]{1,0:T(8,128)} %area.1) | copy-start | bytes 49156
  5.0 18.2 %copy-start.9 = (f32[5,5]{1,0:T(8,128)S(1)}, f32[5,5]{1,0:T(8,128)}, u32[]{:S(2)}) copy-start(f32[5,5]{1,0:T(8,128)} %coupling_ref.1) | copy-start | bytes 304
  23.2 21.5 %copy-start.10 = (f32[4]{0:T(128)S(1)}, f32[4]{0:T(128)}, u32[]{:S(2)}) copy-start(f32[4]{0:T(128)} %param.17) | copy-start | bytes 52
  44.1 0.6 copy-start.8

commit v2 on v0

v2 whole, which is shorter than its diff:
```python
import jax
import jax.numpy as jnp
from jax import lax
from jax.experimental import pallas as pl
from jax.experimental.pallas import tpu as pltpu
from jax.sharding import PartitionSpec as P

STEPS = 4
ACT = 4
FIELDS = 5
ROWS = 64
COLS = 512
LANES = 128
BLOCKS = COLS // LANES
CHUNK = 16
CHUNKS = ROWS // CHUNK
EXT = ROWS + 2 * CHUNK
ORDER = (3, 0, 1, 2)
MESH = pl.DeviceIdType.MESH
LEVELS = 32767.0
f32 = jnp.float32
bf16 = jnp.bfloat16

LEFT = ((3, 13, 39, 5), (2, 14, 38, 4), (1, 15, 37, 4), (0, 16, 36, 4))
RIGHT = ((3, 65, 75, 3), (2, 66, 74, 2), (1, 67, 73, 2), (0, 68, 72, 2))
MIDDLE = ((3, 47, 57, 3), (2, 46, 58, 3), (1, 45, 59, 3), (0, 44, 60, 3))


def quantize(src, piece, dst, row, scales):
    tile = []
    for f in range(FIELDS):
        x = src[f, pl.ds(piece * CHUNK, CHUNK), :]
        top = jnp.max(jnp.abs(x), axis=(0, 1), keepdims=True)
        safe = jnp.maximum(top, 1e-30)
        y = jnp.round(x * (LEVELS / safe))
        dst[f, pl.ds(row, CHUNK), :] = y.astype(jnp.int32).astype(jnp.int16)
        tile.append(jnp.broadcast_to(safe * (1.0 / LEVELS), (1, LANES)))
    tile += [jnp.zeros((1, LANES), f32)] * (8 - FIELDS)
    scales[piece] = jnp.concatenate(tile, axis=0)


def one_tile(src, cond, row, coupling, lane):
    first, last = lane == 0, lane == LANES - 1
    weight = [cond[b, pl.ds(row, 8), :] for b in range(BLOCKS)]
    mixed = []
    for f in range(FIELDS):
        mid = [src[f, b, pl.ds(row, 8), :] for b in range(BLOCKS)]
        left = [pltpu.roll(v, 1, 1) for v in mid]
        right = [pltpu.roll(v, LANES - 1, 1) for v in mid]
        out = []
        for b in range(BLOCKS):
            west = jnp.where(first, left[b - 1] if b else 0.0, left[b])
            east = jnp.where(last, right[b + 1] if b < BLOCKS - 1 else 0.0, right[b])
            north = src[f, b, pl.ds(row - 1, 8), :]
            south = src[f, b, pl.ds(row + 1, 8), :]
            beside = 0.35 * north + 0.15 * south + 0.3 * west + 0.2 * east
            out.append(mid[b] + weight[b] * (beside - mid[b]))
        mixed.append(out)
    result = []
    for f in range(FIELDS):
        row_out = []
        for b in range(BLOCKS):
            total = coupling[0][f] * mixed[0][b]
            for g in range(1, FIELDS):
                total = total + coupling[g][f] * mixed[g][b]
            row_out.append(total)
        result.append(row_out)
    return result


def space_offsets(ns):
    nc = 2
    nx = min(4, ns // nc)
    ny = ns // (nc * nx)
    far = lambda d, n: min(d, n - d)
    steps = [(y, x, c) for y in range(ny) for x in range(nx) for c in range(nc)][1:]
    steps.sort(key=lambda o: -(2 * far(o[0], ny) + 2 * far(o[1], nx) + o[2]))
    return steps, (ny, nx, nc)


def time_offsets(nt):
    return sorted(range(1, nt), key=lambda j: -min(j, nt - j))


def offsets(distances, n):
    return sorted({d % n for d in distances} - {0})


def whole(
    points_in, terminal, forcing, conductance, coupling_ref, cells_in, acts_in, area_in, rate_ref,
    points, states,
    raw, coded, coded_scale, end_scale, start, scale, force_halo, cond_halo,
    force_own, cond_own, cells, acts, area,
    lam, push, cond, column, row_area, energy, picked, partial, mine, later, later_weight, send,
    raw_sem, in_sem, z_send, z_recv, s_send, s_recv, a_send, a_recv, t_send, t_recv,
    greet_y, greet_far, greet_farther,
):
    nt, ns = lax.axis_size("tm"), lax.axis_size("space")
    t, s = lax.axis_index("tm"), lax.axis_index("space")
    around, (ny, nx, nc) = space_offsets(ns)
    place = (s // (nx * nc), lax.rem(s // nc, nx), lax.rem(s, nc))

    def beside(o):
        y, x = lax.rem(place[0] + o[0], ny), lax.rem(place[1] + o[1], nx)
        c = 1 - place[2] if o[2] else place[2]
        return (t, (y * nx + x) * nc + c)

    def inverse(o):
        return around.index(((-o[0]) % ny, (-o[1]) % nx, o[2]))

    def in_time(j):
        return (lax.rem(t + j, nt), s)

    def signal(sem, dev):
        pl.semaphore_signal(sem, inc=1, device_id=dev, device_id_type=MESH)

    raw_loads = [
        pltpu.make_async_copy(
            points_in.at[0, :, pl.ds(p * CHUNK, CHUNK), :], raw.at[:, pl.ds(p * CHUNK, CHUNK), :],
            raw_sem.at[p],
        )
        for p in range(CHUNKS)
    ]
    for p in ORDER:
        raw_loads[p].start()
    later[...] = jnp.zeros(later.shape, f32)
    barrier = pltpu.get_barrier_semaphore()
    near_time = offsets((1, -1, 2, -2), nt)
    near_space = [o for o in around if o[0] == 0 or o[1:] == (0, 0)]
    for j in near_time:
        signal(barrier, in_time(j))
    signal(barrier, (t, lax.rem(s + 1, ns)))
    signal(barrier, (t, lax.rem(s + ns - 1, ns)))
    for o in near_space:
        signal(barrier, beside(o))
    loads = [
        pltpu.make_async_copy(src, dst, in_sem.at[i])
        for i, (src, dst) in enumerate((
            (cells_in, cells), (acts_in, acts), (area_in, area), (conductance, cond_own),
            (forcing.at[0], force_own),
        ))
    ]
    for load in loads:
        load.start()
    for p in ORDER:
        raw_loads[p].wait()
        quantize(raw, p, coded, p * CHUNK, coded_scale)
    pl.semaphore_wait(barrier, len(near_time) + 2 + len(near_space))

    def z_copy(src, dst, i):
        return pltpu.make_async_remote_copy(
            src_ref=src, dst_ref=dst, send_sem=z_send.at[i], recv_sem=z_recv.at[i],
            device_id=(t - 1, s), device_id_type=MESH,
        )

    z_scale = z_copy(coded_scale, scale.at[pl.ds(1, CHUNKS)], CHUNKS)
    z_piece = [
        z_copy(
            coded.at[:, pl.ds(p * CHUNK, CHUNK), :], start.at[:, pl.ds((p + 1) * CHUNK, CHUNK), :], p
        )
        for p in range(CHUNKS)
    ]

    def s_copy(src, dst, i, to):
        return pltpu.make_async_remote_copy(
            src_ref=src, dst_ref=dst, send_sem=s_send.at[i], recv_sem=s_recv.at[i],
            device_id=(t, to), device_id_type=MESH,
        )

    up_first = [
        s_copy(conductance.at[pl.ds(ROWS - 8, 8)], cond_halo.at[0], 0, s + 1),
        s_copy(
            forcing.at[0, pl.ds(1, 3), :, pl.ds(ROWS - CHUNK, CHUNK), :], force_halo.at[0], 1, s + 1
        ),
    ]
    down_first = [
        s_copy(conductance.at[pl.ds(0, 8)], cond_halo.at[1], 4, s - 1),
        s_copy(forcing.at[0, pl.ds(1, 3), :, pl.ds(0, CHUNK), :], force_halo.at[1], 5, s - 1),
    ]
    up_then = [
        s_copy(scale.at[CHUNKS], scale.at[0], 2, s + 1),
        s_copy(start.at[:, pl.ds(ROWS, CHUNK), :], start.at[:, pl.ds(0, CHUNK), :], 3, s + 1),
    ]
    down_then = [
        s_copy(scale.at[1], scale.at[CHUNKS + 1], 6, s - 1),
        s_copy(
            start.at[:, pl.ds(CHUNK, CHUNK), :], start.at[:, pl.ds(ROWS + CHUNK, CHUNK), :], 7, s - 1
        ),
    ]
    has_up, has_down = s < ns - 1, s > 0
    has_later, has_earlier = t < nt - 1, t > 0

    @pl.when(has_earlier)
    def _():
        z_scale.start()
        for p in ORDER:
            z_piece[p].start()

    @pl.when(has_up)
    def _():
        for copy in up_first:
            copy.start()

    @pl.when(has_down)
    def _():
        for copy in down_first:
            copy.start()

    same_x = [o for o in near_space if o[1:] == (0, 0)]
    for o in same_x:
        signal(greet_y, beside(o))
    far = offsets((2, -2), nt)
    for j in far:
        signal(greet_far, in_time(j))

    @pl.when(jnp.logical_not(has_later))
    def _():
        end = pltpu.make_async_copy(terminal, raw, raw_sem.at[0])
        end.start()
        end.wait()
        for p in range(CHUNKS):
            quantize(raw, p, start, (p + 1) * CHUNK, end_scale)
            scale[p + 1] = end_scale[p]

    for load in loads:
        load.wait()

    def slots(p, carry):
        for half in range(2):
            cell = cells[pl.ds(2 * p + half, 1), :]
            lanes = pl.ds(half * LANES, LANES)
            col = jnp.broadcast_to(jnp.bitwise_and(cell, COLS - 1), (COLS, LANES))
            at = lax.broadcasted_iota(jnp.int32, (COLS, LANES), 0)
            column[p, :, lanes] = jnp.where(col == at, 1.0, 0.0).astype(bf16)
            row = jnp.broadcast_to(lax.shift_right_arithmetic(cell, 9), (ROWS, LANES))
            weight = jnp.broadcast_to(area[pl.ds(2 * p + half, 1), :], (ROWS, LANES))
            at = lax.broadcasted_iota(jnp.int32, (ROWS, LANES), 0)
            row_area[p, :, lanes] = jnp.where(row == at, weight, 0.0)
        return carry

    lax.fori_loop(0, ns // 2, slots, 0)

    def widen(i, carry):
        k, f = i // FIELDS, lax.rem(i, FIELDS)
        value = force_own[k, f].astype(f32)
        for b in range(BLOCKS):
            push[k, f, b, pl.ds(CHUNK, ROWS), :] = value[:, b * LANES : (b + 1) * LANES]
        return carry

    lax.fori_loop(0, STEPS * FIELDS, widen, 0)
    for b in range(BLOCKS):
        cond[b, pl.ds(CHUNK, ROWS), :] = cond_own[:, pl.ds(b * LANES, LANES)]

    lane1 = lax.broadcasted_iota(jnp.int32, (1, LANES), 1)
    rate = jnp.zeros((1, LANES), f32)
    for a in range(ACT):
        rate = jnp.where(lax.rem(lane1, ACT) == a, rate_ref[a], rate)
    for j in range(1, nt):
        later_weight[j] = jnp.exp(-float(STEPS * (j - 1)) * rate)
    later_weight[0] = jnp.zeros((1, LANES), f32)

    lane = lax.broadcasted_iota(jnp.int32, (8, LANES), 1)
    coupling = [[coupling_ref[g, f] for f in range(FIELDS)] for g in range(FIELDS)]

    def decode(piece):
        rows = pl.ds(piece * CHUNK, CHUNK)
        for f in range(FIELDS):
            value = start[f, rows, :].astype(jnp.int32).astype(f32)
            factor = scale[piece, f : f + 1, :]
            for b in range(BLOCKS):
                lam[0, f, b, rows, :] = value[:, b * LANES : (b + 1) * LANES] * factor

    def windows(parts):
        for k, first, last, count in parts:
            def body(i, carry, k=k, first=first, last=last):
                row = jnp.minimum(first + 8 * i, last)
                got = one_tile(lam.at[STEPS - 1 - k], cond, row, coupling, lane)
                for f in range(FIELDS):
                    for b in range(BLOCKS):
                        lam[STEPS - k, f, b, pl.ds(row, 8), :] = (
                            got[f][b] + push[k, f, b, pl.ds(row, 8), :]
                        )
                return carry

            lax.fori_loop(0, count, body, 0)

    @pl.when(has_later)
    def _():
        z_scale.wait_recv()
        z_piece[3].wait_recv()

    @pl.when(has_up)
    def _():
        for copy in up_then:
            copy.start()

    decode(4)

    @pl.when(has_later)
    def _():
        z_piece[0].wait_recv()

    @pl.when(has_down)
    def _():
        for copy in down_then:
            copy.start()

    decode(1)
    pl.semaphore_wait(greet_far, len(far))
    farther = offsets((4, -4), nt)
    for j in farther:
        signal(greet_farther, in_time(j))

    @pl.when(jnp.logical_not(has_down))
    def _():
        cond_halo[0] = jnp.zeros((8, COLS), f32)
        force_halo[0] = jnp.zeros((3, FIELDS, CHUNK, COLS), bf16)
        scale[0] = jnp.zeros((8, LANES), f32)
        start[:, pl.ds(0, CHUNK), :] = jnp.zeros((FIELDS, CHUNK, COLS), jnp.int16)

    @pl.when(jnp.logical_not(has_up))
    def _():
        cond_halo[1] = jnp.zeros((8, COLS), f32)
        force_halo[1] = jnp.zeros((3, FIELDS, CHUNK, COLS), bf16)
        scale[CHUNKS + 1] = jnp.zeros((8, LANES), f32)
        start[:, pl.ds(ROWS + CHUNK, CHUNK), :] = jnp.zeros((FIELDS, CHUNK, COLS), jnp.int16)

    @pl.when(has_down)
    def _():
        for copy in up_first:
            copy.wait_recv()

    @pl.when(has_up)
    def _():
        for copy in down_first:
            copy.wait_recv()

    for edge, row in ((0, 8), (1, CHUNK + ROWS)):
        for b in range(BLOCKS):
            cond[b, pl.ds(row, 8), :] = cond_halo[edge, :, pl.ds(b * LANES, LANES)]
        for k in range(1, STEPS):
            for f in range(FIELDS):
                value = force_halo[edge, k - 1, f].astype(f32)
                value = value[8:] if edge == 0 else value[:8]
                for b in range(BLOCKS):
                    push[k, f, b, pl.ds(row, 8), :] = value[:, b * LANES : (b + 1) * LANES]

    @pl.when(has_later)
    def _():
        z_piece[1].wait_recv()

    decode(2)

    @pl.when(has_down)
    def _():
        for copy in up_then:
            copy.wait_recv()

    decode(0)
    windows(LEFT)

    @pl.when(has_up)
    def _():
        for copy in down_then:
            copy.wait_recv()

    decode(5)
    windows(RIGHT)

    @pl.when(has_later)
    def _():
        z_piece[2].wait_recv()

    decode(3)
    windows(MIDDLE)

    out = []
    for b in range(BLOCKS):
        copy = pltpu.make_async_copy(
            lam.at[STEPS, :, b, pl.ds(CHUNK, ROWS), :], points.at[0, :, :, pl.ds(b * LANES, LANES)],
            raw_sem.at[b],
        )
        copy.start()
        out.append(copy)
    for k in range(STEPS):
        value = jnp.concatenate(
            [lam[STEPS - k, 4, b, pl.ds(CHUNK, ROWS), :] for b in range(BLOCKS)], axis=1
        )
        high = value.astype(bf16)
        energy[pl.ds(2 * k * ROWS, ROWS), :] = high
        energy[pl.ds((2 * k + 1) * ROWS, ROWS), :] = (value - high.astype(f32)).astype(bf16)

    def pick(p, carry):
        got = jnp.dot(energy[...], column[p], preferred_element_type=f32)
        weight = row_area[p]
        for k in range(STEPS):
            at = 2 * k * ROWS
            both = (got[at : at + ROWS] + got[at + ROWS : at + 2 * ROWS]) * weight
            line = jnp.sum(both, axis=0, keepdims=True)
            for half in range(2):
                picked[k, pl.ds(2 * p + half, 1), :] = line[:, half * LANES : (half + 1) * LANES]
        return carry

    lax.fori_loop(0, ns // 2, pick, 0)
    ids = acts[...]
    wide = lax.broadcasted_iota(jnp.int32, ids.shape, 1)
    total = jnp.zeros(ids.shape, f32)
    for k in range(STEPS):
        values = picked[k]
        for a in range(ACT):
            part = jnp.sum(jnp.where(ids == a, values, 0.0), axis=1, keepdims=True)
            total = jnp.where(jnp.bitwise_and(wide, STEPS * ACT - 1) == k * ACT + a, part, total)
    partial[...] = total.reshape(partial.shape)

    pl.semaphore_wait(greet_y, len(same_x))
    to_owner = []
    for i, o in enumerate(around):
        dev = beside(o)
        to_owner.append(pltpu.make_async_remote_copy(
            src_ref=partial.at[dev[1]], dst_ref=mine.at[inverse(o)],
            send_sem=a_send.at[i], recv_sem=a_recv.at[inverse(o)],
            device_id=dev, device_id_type=MESH,
        ))
    for copy in to_owner:
        copy.start()
    mine[ns - 1] = partial[s]
    k_of = lax.rem(lane1, STEPS * ACT) // ACT
    k_f = k_of.astype(f32)
    decay = [jnp.exp(-float(m) * rate) for m in range(STEPS)]
    pl.semaphore_wait(greet_farther, len(farther))
    for i, o in enumerate(around):
        pltpu.make_async_remote_copy(
            src_ref=partial.at[s], dst_ref=mine.at[i], send_sem=a_send.at[i], recv_sem=a_recv.at[i],
            device_id=beside(o), device_id_type=MESH,
        ).wait_recv()
    load = jnp.sum(mine[...], axis=0)
    weighted = load * jnp.exp(-k_f * rate)
    for shift in (8, 4):
        weighted = weighted + pltpu.roll(weighted, shift, 1)
    send[...] = weighted

    to_earlier = {
        j: pltpu.make_async_remote_copy(
            src_ref=send, dst_ref=later.at[j], send_sem=t_send.at[j], recv_sem=t_recv.at[j],
            device_id=(t - j, s), device_id_type=MESH,
        )
        for j in time_offsets(nt)
    }
    for j, copy in to_earlier.items():
        pl.when(t >= j)(copy.start)
    base = load
    for m in range(1, STEPS):
        moved = pltpu.roll(load, LANES - ACT * m, 1)
        base = base + jnp.where(k_of + m < STEPS, decay[m] * moved, 0.0)
    for j, copy in to_earlier.items():
        pl.when(t + j < nt)(copy.wait_recv)
    incoming = jnp.sum(later[...] * later_weight[...], axis=0)
    result = base + jnp.exp(-(STEPS - k_f) * rate) * incoming
    for k in range(STEPS):
        moved = pltpu.roll(result, LANES - ACT * k, 1) if k else result
        states[0, pl.ds(k, 1), :] = moved[:, :ACT]

    for j, copy in to_earlier.items():
        pl.when(t >= j)(copy.wait_send)
    for copy in to_owner:
        copy.wait_send()

    @pl.when(has_up)
    def _():
        for copy in up_first + up_then:
            copy.wait_send()

    @pl.when(has_down)
    def _():
        for copy in down_first + down_then:
            copy.wait_send()

    @pl.when(has_earlier)
    def _():
        z_scale.wait_send()
        for copy in z_piece:
            copy.wait_send()

    for copy in out:
        copy.wait()


def per_device(
    c_points, terminal, forcing, conductance, coupling, flap_cells, flap_actuator, flap_area, actuator_rate
):
    nt, ns = lax.axis_size("tm"), lax.axis_size("space")
    anywhere = pl.BlockSpec(memory_space=pl.ANY)
    vmem = pl.BlockSpec(memory_space=pltpu.VMEM)
    smem = pl.BlockSpec(memory_space=pltpu.SMEM)
    dma = pltpu.SemaphoreType.DMA
    regular = pltpu.SemaphoreType.REGULAR
    i32 = jnp.int32
    points, states = pl.pallas_call(
        whole,
        out_shape=(
            jax.ShapeDtypeStruct((1, FIELDS, ROWS, COLS), f32),
            jax.ShapeDtypeStruct((1, STEPS, ACT), f32),
        ),
        in_specs=[anywhere] * 4 + [smem] + [anywhere] * 3 + [smem],
        out_specs=(anywhere, vmem),
        scratch_shapes=[
            pltpu.VMEM((FIELDS, ROWS, COLS), f32),
            pltpu.VMEM((FIELDS, ROWS, COLS), jnp.int16),
            pltpu.VMEM((CHUNKS, 8, LANES), f32),
            pltpu.VMEM((CHUNKS, 8, LANES), f32),
            pltpu.VMEM((FIELDS, EXT, COLS), jnp.int16),
            pltpu.VMEM((CHUNKS + 2, 8, LANES), f32),
            pltpu.VMEM((2, STEPS - 1, FIELDS, CHUNK, COLS), bf16),
            pltpu.VMEM((2, 8, COLS), f32),
            pltpu.VMEM((STEPS, FIELDS, ROWS, COLS), bf16),
            pltpu.VMEM((ROWS, COLS), f32),
            pltpu.VMEM((ns, LANES), i32),
            pltpu.VMEM((ns, LANES), i32),
            pltpu.VMEM((ns, LANES), f32),
            pltpu.VMEM((STEPS + 1, FIELDS, BLOCKS, EXT, LANES), f32),
            pltpu.VMEM((STEPS, FIELDS, BLOCKS, EXT, LANES), f32),
            pltpu.VMEM((BLOCKS, EXT, LANES), f32),
            pltpu.VMEM((ns // 2, COLS, 2 * LANES), bf16),
            pltpu.VMEM((ns // 2, ROWS, 2 * LANES), f32),
            pltpu.VMEM((2 * STEPS * ROWS, COLS), bf16),
            pltpu.VMEM((STEPS, ns, LANES), f32),
            pltpu.VMEM((ns, 1, LANES), f32),
            pltpu.VMEM((ns, 1, LANES), f32),
            pltpu.VMEM((nt, 1, LANES), f32),
            pltpu.VMEM((nt, 1, LANES), f32),
            pltpu.VMEM((1, LANES), f32),
            dma((CHUNKS,)), dma((5,)), dma((CHUNKS + 1,)), dma((CHUNKS + 1,)), dma((8,)), dma((8,)),
            dma((ns,)), dma((ns,)), dma((nt,)), dma((nt,)),
            regular, regular, regular,
        ],
        compiler_params=pltpu.CompilerParams(
            collective_id=0, has_side_effects=True, vmem_limit_bytes=60 * 2**20
        ),
        name="whole",
    )(c_points, terminal, forcing, conductance, coupling, flap_cells, flap_actuator, flap_area, actuator_rate)
    return (points, states)


def solution(mesh):
    placed = (
        P("tm", None, "space", None),
        P(None, "space", None),
        P("tm", None, None, "space", None),
        P("space", None),
        P(),
        P("space", None),
        P("space", None),
        P("space", None),
        P("space"),
    )
    return jax.shard_map(
        per_device,
        mesh=mesh,
        in_specs=placed,
        out_specs=(P("tm", None, "space", None), P("tm", None, "space")),
        check_vma=False,
    )
```

time: 216 us -> 49.4 us (0.23)
  the two profiles are of different devices: /device:TPU:8 before, /device:TPU:1 now
where the time goes in v2:
time: 49.4 us; the launch traced here: 49.2 us
  Pallas kernels  46 us (93%)
  local copies, waits for them, and re-layouts  2.57 us (5%)
  between operations  0.65 us (1%)
    pallas_call x1, Pallas kernels, per_device(): pl.pallas_call(whole, out_shape=(jax.ShapeDtypeStruct((1, FIELDS, ROWS, C...  46 us
    unnamed x4, local copies, waits for them, and re-layouts  2.57 us

profile of v2, /device:TPU:1, one launch (start us, length us, event | category | flops | bytes accessed | tf_op | source)
XLA Modules:
  0.0 49.2 jit_solution(6071696204315896319)
XLA Ops:
  0.6 46.0 %whole.1 = (f32[1,5,64,512]{3,2,1,0:T(8,128)}, f32[1,4,4]{2,1,0:T(4,128)}) custom-call(f32[1,5,64,512]{3,2,1,0:T(8,128)} %points_in.1, f32[5,64,512]{2,1,0:T(8,128)} %terminal.1, bf16[1,4,5,64,512]{4,3,2,1,0:T(8,128)(2,1)} %forcing.1, f32[64,512]{1,0:T(8,128)} %conductance.1, f32[5,5]{1,0:T(8,128)} %coupling_ref.1, s32[32,128]{1,0:T(8,128)} %cells_in.1, ...), custom_call_target="tpu_custom_call" | custom-call | tf_op jit(solution)/shard_map/whole/pallas_call | solution.py:498
  46.6 0.0 copy-start
  46.6 2.0 %copy.13 = f32[1,5,64,512]{3,2,1,0:T(8,128)} copy(f32[1,5,64,512]{3,2,1,0:T(8,128)} %get-tuple-element.4) | data formatting | bytes 1310720
  48.6 0.0 copy-done
  48.6 0.6 %copy.14 = f32[1,4,4]{2,1,0:T(4,128)} copy(f32[1,4,4]{2,1,0:T(4,128)S(1)} %copy-done) | data formatting | bytes 128
Async XLA Ops:
  46.6 2.0 %copy-start = (f32[1,4,4]{2,1,0:T(4,128)S(1)}, f32[1,4,4]{2,1,0:T(4,128)}, u32[]{:S(2)}) copy-start(f32[1,4,4]{2,1,0:T(4,128)} %get-tuple-element.5) | copy-start | bytes 196

commit v3 on v0

v3 whole, which is shorter than its diff:
```python
import jax
import jax.numpy as jnp
from jax import lax
from jax.experimental import pallas as pl
from jax.experimental.pallas import tpu as pltpu
from jax.sharding import PartitionSpec as P

STEPS = 4
ACT = 4
FIELDS = 5
ROWS = 64
COLS = 512
LANES = 128
BLOCKS = COLS // LANES
EDGE = 16
EXT = ROWS + 2 * EDGE
PIECE = 16
PIECES = ROWS // PIECE
GROUP = STEPS * ACT
SETS = 2 * STEPS
MESH = pl.DeviceIdType.MESH
LEVELS = 32767.0
f32 = jnp.float32
bf16 = jnp.bfloat16


def pair(ref, f, b, rows, shift):
    return jnp.concatenate([ref[f, b, pl.ds(row + shift, 8), :] for row in rows], axis=0)


def step_map(src, cond, rows, coupling, lane):
    first, last = lane == 0, lane == LANES - 1
    weight = [
        jnp.concatenate([cond[b, pl.ds(row, 8), :] for row in rows], axis=0) for b in range(BLOCKS)
    ]
    none = jnp.zeros(lane.shape, bf16)
    mixed = []
    for f in range(FIELDS):
        mid = [pair(src, f, b, rows, 0) for b in range(BLOCKS)]
        short = [v.astype(bf16) for v in mid]
        left = [pltpu.roll(v, 1, 1) for v in short]
        right = [pltpu.roll(v, LANES - 1, 1) for v in short]
        out = []
        for b in range(BLOCKS):
            west = jnp.where(first, left[b - 1] if b else none, left[b])
            east = jnp.where(last, right[b + 1] if b < BLOCKS - 1 else none, right[b])
            flat = (jnp.bfloat16(3.0) * west + jnp.bfloat16(2.0) * east).astype(f32)
            north, south = pair(src, f, b, rows, -1), pair(src, f, b, rows, 1)
            beside = 0.35 * north + 0.15 * south + 0.1 * flat
            out.append(mid[b] + weight[b] * (beside - mid[b]))
        mixed.append(out)
    result = []
    for f in range(FIELDS):
        row_out = []
        for b in range(BLOCKS):
            total = coupling[0][f] * mixed[0][b]
            for g in range(1, FIELDS):
                total = total + coupling[g][f] * mixed[g][b]
            row_out.append(total)
        result.append(row_out)
    return result


def space_offsets(ns):
    nc = 2
    nx = min(4, ns // nc)
    ny = ns // (nc * nx)
    far = lambda d, n: min(d, n - d)
    steps = [(y, x, c) for y in range(ny) for x in range(nx) for c in range(nc)][1:]
    steps.sort(key=lambda o: -(2 * far(o[0], ny) + 2 * far(o[1], nx) + o[2]))
    return steps, (ny, nx, nc)


def time_offsets(nt):
    return sorted(range(1, nt), key=lambda j: -min(j, nt - j))


def offsets(distances, n):
    return sorted({d % n for d in distances} - {0})


def whole(
    points_in, terminal, forcing, conductance, coupling_ref, cells_in, acts_in, area_in, rate_ref,
    points, states,
    free, forced, push, cond, force_own, force_out, force_in, cells, acts, area,
    coded, coded_scale, got, got_scale,
    column, row_area, energy, picked, partial, mine, later, later_weight, send,
    in_sem, z_send, z_recv, s_send, s_recv, a_send, a_recv, t_send, t_recv,
    greet_y, greet_far, greet_farther,
):
    nt, ns = lax.axis_size("tm"), lax.axis_size("space")
    t, s = lax.axis_index("tm"), lax.axis_index("space")
    around, (ny, nx, nc) = space_offsets(ns)
    place = (s // (nx * nc), lax.rem(s // nc, nx), lax.rem(s, nc))
    has_up, has_down = s < ns - 1, s > 0
    has_later, has_earlier = t < nt - 1, t > 0
    is_last = jnp.logical_not(has_later)

    def beside(o):
        y, x = lax.rem(place[0] + o[0], ny), lax.rem(place[1] + o[1], nx)
        c = 1 - place[2] if o[2] else place[2]
        return (t, (y * nx + x) * nc + c)

    def inverse(o):
        return around.index(((-o[0]) % ny, (-o[1]) % nx, o[2]))

    def in_time(j):
        return (lax.rem(t + j, nt), s)

    def signal(sem, dev):
        pl.semaphore_signal(sem, inc=1, device_id=dev, device_id_type=MESH)

    own = pl.ds(EDGE, ROWS)

    def load(src, dst, i):
        return pltpu.make_async_copy(src, dst, in_sem.at[i])

    def columns(src, dst, i):
        return [
            load(
                src.at[..., pl.ds(b * LANES, LANES)],
                dst.at[:, b, own, :] if len(dst.shape) == 4 else dst.at[b, own, :], i + b,
            )
            for b in range(BLOCKS)
        ]

    first_loads = columns(points_in.at[0], free.at[0], 0) + columns(conductance, cond, 4)
    force_load = load(forcing.at[0], force_own, 8)
    slot_loads = [load(cells_in, cells, 9), load(acts_in, acts, 10), load(area_in, area, 11)]
    end_loads = columns(terminal, forced.at[0], 12)
    for copy in first_loads + [force_load] + slot_loads:
        copy.start()

    @pl.when(is_last)
    def _():
        for copy in end_loads:
            copy.start()

    later[...] = jnp.zeros(later.shape, f32)
    barrier = pltpu.get_barrier_semaphore()
    near_time = offsets((1, -1, 2, -2), nt)
    near_space = [o for o in around if o[0] == 0 or o[1:] == (0, 0)]
    for j in near_time:
        signal(barrier, in_time(j))
    signal(barrier, (t, lax.rem(s + 1, ns)))
    signal(barrier, (t, lax.rem(s + ns - 1, ns)))
    for o in near_space:
        signal(barrier, beside(o))

    lane16 = lax.broadcasted_iota(jnp.int32, (16, LANES), 1)
    lane1 = lax.broadcasted_iota(jnp.int32, (1, LANES), 1)
    coupling = [[coupling_ref[g, f] for f in range(FIELDS)] for g in range(FIELDS)]

    def advance(src, add, dst, rows):
        value = step_map(src, cond, rows, coupling, lane16)
        for f in range(FIELDS):
            for b in range(BLOCKS):
                for half, row in enumerate(rows):
                    part = value[f][b][8 * half : 8 * half + 8]
                    if add is not None:
                        part = part + add[f, b, pl.ds(row, 8), :]
                    dst[f, b, pl.ds(row, 8), :] = part

    def interior(src, add, dst, j):
        def body(i, carry):
            row = jnp.minimum(EDGE + j + 16 * i, EDGE + ROWS - j - 16)
            advance(src, add, dst, (row, row + 8))
            return carry

        lax.fori_loop(0, ROWS // 16, body, 0)

    def edges(src, add, dst, j):
        advance(src, add, dst, (EDGE - 4 + j, EDGE + ROWS - 4 - j))

    for copy in first_loads:
        copy.wait()
    interior(free.at[0], None, free.at[1], 1)
    interior(free.at[1], None, free.at[2], 2)

    force_load.wait()
    for side, at in ((0, 13), (1, 0)):
        for f in range(FIELDS):
            for k, count, to in ((3, 3, 0), (2, 2, 3), (1, 1, 5)):
                near = force_own[k, f, pl.ds(ROWS - 16 if side == 0 else 0, 16), :].astype(f32)
                near = near[16 - count :] if side == 0 else near[:count]
                for b in range(BLOCKS):
                    force_out[side, f, b, pl.ds(to, count), :] = near[:, b * LANES : (b + 1) * LANES]
            for b in range(BLOCKS):
                force_out[side, f, b, pl.ds(6, 2), :] = jnp.zeros((2, LANES), f32)

    @pl.when(jnp.logical_not(has_down))
    def _():
        free[0, :, :, pl.ds(8, 8), :] = jnp.zeros((FIELDS, BLOCKS, 8, LANES), f32)
        forced[0, :, :, pl.ds(8, 8), :] = jnp.zeros((FIELDS, BLOCKS, 8, LANES), f32)
        cond[:, pl.ds(8, 8), :] = jnp.zeros((BLOCKS, 8, LANES), f32)
        force_in[0] = jnp.zeros((FIELDS, BLOCKS, 8, LANES), f32)

    @pl.when(jnp.logical_not(has_up))
    def _():
        high = pl.ds(EDGE + ROWS, 8)
        free[0, :, :, high, :] = jnp.zeros((FIELDS, BLOCKS, 8, LANES), f32)
        forced[0, :, :, high, :] = jnp.zeros((FIELDS, BLOCKS, 8, LANES), f32)
        cond[:, high, :] = jnp.zeros((BLOCKS, 8, LANES), f32)
        force_in[1] = jnp.zeros((FIELDS, BLOCKS, 8, LANES), f32)

    @pl.when(is_last)
    def _():
        for copy in end_loads:
            copy.wait()

    pl.semaphore_wait(barrier, len(near_time) + 2 + len(near_space))

    def s_copy(src, dst, i, to):
        return pltpu.make_async_remote_copy(
            src_ref=src, dst_ref=dst, send_sem=s_send.at[i], recv_sem=s_recv.at[i],
            device_id=(t, to), device_id_type=MESH,
        )

    def halo(side):
        to = s + 1 if side == 0 else s - 1
        mine_rows = pl.ds(EDGE + ROWS - 8 if side == 0 else EDGE, 8)
        their_rows = pl.ds(8 if side == 0 else EDGE + ROWS, 8)
        i = 4 * side
        return [
            s_copy(free.at[0, :, :, mine_rows, :], free.at[0, :, :, their_rows, :], i, to),
            s_copy(cond.at[:, mine_rows, :], cond.at[:, their_rows, :], i + 1, to),
            s_copy(force_out.at[side], force_in.at[side], i + 2, to),
            s_copy(forced.at[0, :, :, mine_rows, :], forced.at[0, :, :, their_rows, :], i + 3, to),
        ]

    up, down = halo(0), halo(1)
    for has, copies in ((has_up, up), (has_down, down)):
        @pl.when(has)
        def _(copies=copies):
            for copy in copies[:3]:
                copy.start()

        @pl.when(jnp.logical_and(has, is_last))
        def _(copies=copies):
            copies[3].start()

    same_x = [o for o in near_space if o[1:] == (0, 0)]
    for o in same_x:
        signal(greet_y, beside(o))
    far = offsets((2, -2), nt)
    for j in far:
        signal(greet_far, in_time(j))

    interior(free.at[2], None, free.at[3], 3)
    interior(free.at[3], None, free.at[4], 4)

    def widen(i, carry):
        k, f = i // FIELDS, lax.rem(i, FIELDS)
        value = force_own[k, f].astype(f32)
        for b in range(BLOCKS):
            push[k, f, b, own, :] = value[:, b * LANES : (b + 1) * LANES]
        return carry

    lax.fori_loop(0, STEPS * FIELDS, widen, 0)

    @pl.when(has_later)
    def _():
        forced[1, :, :, own, :] = push[3, :, :, own, :]

    @pl.when(is_last)
    def _():
        interior(forced.at[0], push.at[3], forced.at[1], 1)

    pl.semaphore_wait(greet_far, len(far))
    farther = offsets((4, -4), nt)
    for j in farther:
        signal(greet_farther, in_time(j))

    for j in range(2, STEPS + 1):
        interior(forced.at[j - 1], push.at[STEPS - j], forced.at[j], j)

    for copy in slot_loads:
        copy.wait()

    def slots(p, carry):
        for half in range(2):
            cell = cells[pl.ds(2 * p + half, 1), :]
            lanes = pl.ds(half * LANES, LANES)
            col = jnp.broadcast_to(jnp.bitwise_and(cell, COLS - 1), (COLS, LANES))
            at = lax.broadcasted_iota(jnp.int32, (COLS, LANES), 0)
            column[p, :, lanes] = jnp.where(col == at, 1.0, 0.0).astype(bf16)
            row = jnp.broadcast_to(lax.shift_right_arithmetic(cell, 9), (ROWS, LANES))
            weight = jnp.broadcast_to(area[pl.ds(2 * p + half, 1), :], (ROWS, LANES))
            at = lax.broadcasted_iota(jnp.int32, (ROWS, LANES), 0)
            row_area[p, :, lanes] = jnp.where(row == at, weight, 0.0)
        return carry

    lax.fori_loop(0, ns // 2, slots, 0)

    for has, copies in ((has_down, up), (has_up, down)):
        @pl.when(has)
        def _(copies=copies):
            for copy in copies[:3]:
                copy.wait_recv()

        @pl.when(jnp.logical_and(has, is_last))
        def _(copies=copies):
            copies[3].wait_recv()

    for side in range(2):
        for k, count, at in ((3, 3, 0), (2, 2, 3), (1, 1, 5)):
            row = EDGE - count if side == 0 else EDGE + ROWS
            push[k, :, :, pl.ds(row, count), :] = force_in[side, :, :, pl.ds(at, count), :]

    for j in range(1, STEPS + 1):
        edges(free.at[j - 1], None, free.at[j], j)

    for piece in range(PIECES):
        tile = []
        for f in range(FIELDS):
            x = free[STEPS, f, :, pl.ds(EDGE + piece * PIECE, PIECE), :]
            top = jnp.max(jnp.abs(x), axis=(0, 1, 2), keepdims=True)
            safe = jnp.maximum(top, 1e-30)
            y = jnp.round(x * (LEVELS / safe))
            coded[f, :, pl.ds(piece * PIECE, PIECE), :] = y.astype(jnp.int32).astype(jnp.int16)
            tile.append(jnp.broadcast_to(safe[0] * (1.0 / LEVELS), (1, LANES)))
        tile += [jnp.zeros((1, LANES), f32)] * (8 - FIELDS)
        coded_scale[piece] = jnp.concatenate(tile, axis=0)

    def z_copy(src, dst, i):
        return pltpu.make_async_remote_copy(
            src_ref=src, dst_ref=dst, send_sem=z_send.at[i], recv_sem=z_recv.at[i],
            device_id=(t - 1, s), device_id_type=MESH,
        )

    z_copies = [z_copy(coded_scale, got_scale, 0), z_copy(coded, got, 1)]

    @pl.when(has_earlier)
    def _():
        for copy in z_copies:
            copy.start()

    @pl.when(has_later)
    def _():
        for row, count, at in ((EDGE - 3, 3, 0), (EDGE + ROWS, 3, 0)):
            forced[1, :, :, pl.ds(row, count), :] = push[3, :, :, pl.ds(row, count), :]

    @pl.when(is_last)
    def _():
        edges(forced.at[0], push.at[3], forced.at[1], 1)

    for j in range(2, STEPS + 1):
        edges(forced.at[j - 1], push.at[STEPS - j], forced.at[j], j)

    for part, ref in enumerate((forced, free)):
        for k in range(STEPS):
            value = jnp.concatenate([ref[STEPS - k, 4, b, own, :] for b in range(BLOCKS)], axis=1)
            high = value.astype(bf16)
            at = 2 * (part * STEPS + k) * ROWS
            energy[pl.ds(at, ROWS), :] = high
            energy[pl.ds(at + ROWS, ROWS), :] = (value - high.astype(f32)).astype(bf16)

    def pick(p, carry):
        out = jnp.dot(energy[...], column[p], preferred_element_type=f32)
        weight = row_area[p]
        for k in range(SETS):
            at = 2 * k * ROWS
            both = (out[at : at + ROWS] + out[at + ROWS : at + 2 * ROWS]) * weight
            line = jnp.sum(both, axis=0, keepdims=True)
            for half in range(2):
                picked[k, pl.ds(2 * p + half, 1), :] = line[:, half * LANES : (half + 1) * LANES]
        return carry

    lax.fori_loop(0, ns // 2, pick, 0, unroll=4 if ns >= 8 else 1)
    ids = acts[...]
    wide = jnp.bitwise_and(lax.broadcasted_iota(jnp.int32, ids.shape, 1), 2 * GROUP - 1)
    total = jnp.zeros(ids.shape, f32)
    for k in range(SETS):
        values = picked[k]
        for a in range(ACT):
            part = jnp.sum(jnp.where(ids == a, values, 0.0), axis=1, keepdims=True)
            total = jnp.where(wide == k * ACT + a, part, total)
    partial[...] = total.reshape(partial.shape)

    pl.semaphore_wait(greet_y, len(same_x))
    to_owner = []
    for i, o in enumerate(around):
        dev = beside(o)
        to_owner.append(pltpu.make_async_remote_copy(
            src_ref=partial.at[dev[1]], dst_ref=mine.at[inverse(o)],
            send_sem=a_send.at[i], recv_sem=a_recv.at[inverse(o)],
            device_id=dev, device_id_type=MESH,
        ))
    for copy in to_owner:
        copy.start()
    mine[ns - 1] = partial[s]

    rate = jnp.zeros((1, LANES), f32)
    for a in range(ACT):
        rate = jnp.where(lax.rem(lane1, ACT) == a, rate_ref[a], rate)
    k_of = lax.rem(lane1, GROUP) // ACT
    k_f = k_of.astype(f32)
    q_of = lane1 // GROUP
    decay = [jnp.exp(-float(m) * rate) for m in range(STEPS)]
    later_weight[0] = jnp.zeros((1, LANES), f32)
    for j in range(1, nt):
        forced_part = jnp.exp(-float(STEPS * (j - 1)) * rate)
        start_part = jnp.exp(-float(STEPS * (j - 2)) * rate) if j > 1 else 0.0
        row = jnp.where(q_of == 0, forced_part, 0.0) + jnp.where(q_of == 1, start_part, 0.0)
        if j == 1:
            row = row + jnp.where(q_of == 5, 1.0, 0.0)
        later_weight[j] = row
    pl.semaphore_wait(greet_farther, len(farther))
    for i, o in enumerate(around):
        pltpu.make_async_remote_copy(
            src_ref=partial.at[s], dst_ref=mine.at[i], send_sem=a_send.at[i], recv_sem=a_recv.at[i],
            device_id=beside(o), device_id_type=MESH,
        ).wait_recv()
    loads = jnp.sum(mine[...], axis=0)
    summed = loads * jnp.exp(-k_f * rate)
    for shift, low in ((8, k_of < 2), (4, lax.rem(k_of, 2) == 0)):
        other = jnp.where(low, pltpu.roll(summed, LANES - shift, 1), pltpu.roll(summed, shift, 1))
        summed = summed + other
    send[...] = jnp.where(q_of < 4, summed, loads)

    to_earlier = {
        j: pltpu.make_async_remote_copy(
            src_ref=send, dst_ref=later.at[j], send_sem=t_send.at[j], recv_sem=t_recv.at[j],
            device_id=(t - j, s), device_id_type=MESH,
        )
        for j in time_offsets(nt)
    }
    for j, copy in to_earlier.items():
        pl.when(t >= j)(copy.start)

    @pl.when(has_later)
    def _():
        for copy in z_copies:
            copy.wait_recv()

    @pl.when(is_last)
    def _():
        got[...] = jnp.zeros(got.shape, jnp.int16)
        got_scale[...] = jnp.zeros(got_scale.shape, f32)

    for piece in range(PIECES):
        rows = pl.ds(piece * PIECE, PIECE)
        for f in range(FIELDS):
            factor = got_scale[piece, f : f + 1, :]
            for b in range(BLOCKS):
                value = got[f, b, rows, :].astype(jnp.int32).astype(f32) * factor
                points[0, f, rows, pl.ds(b * LANES, LANES)] = (
                    value + forced[STEPS, f, b, pl.ds(EDGE + piece * PIECE, PIECE), :]
                )

    for j, copy in to_earlier.items():
        pl.when(t + j < nt)(copy.wait_recv)
    arrived = jnp.sum(later[...] * later_weight[...], axis=0)
    loads = loads + pltpu.roll(arrived, LANES - 5 * GROUP, 1)
    incoming = arrived + pltpu.roll(arrived, LANES - GROUP, 1)
    result = loads + jnp.exp(-(STEPS - k_f) * rate) * incoming
    for m in range(1, STEPS):
        moved = pltpu.roll(loads, LANES - ACT * m, 1)
        result = result + jnp.where(k_of + m < STEPS, decay[m] * moved, 0.0)
    for k in range(STEPS):
        moved = pltpu.roll(result, LANES - ACT * k, 1) if k else result
        states[0, pl.ds(k, 1), :] = moved[:, :ACT]

    for j, copy in to_earlier.items():
        pl.when(t >= j)(copy.wait_send)
    for copy in to_owner:
        copy.wait_send()
    for has, copies in ((has_up, up), (has_down, down)):
        @pl.when(has)
        def _(copies=copies):
            for copy in copies[:3]:
                copy.wait_send()

        @pl.when(jnp.logical_and(has, is_last))
        def _(copies=copies):
            copies[3].wait_send()

    @pl.when(has_earlier)
    def _():
        for copy in z_copies:
            copy.wait_send()


def per_device(
    c_points, terminal, forcing, conductance, coupling, flap_cells, flap_actuator, flap_area, actuator_rate
):
    nt, ns = lax.axis_size("tm"), lax.axis_size("space")
    anywhere = pl.BlockSpec(memory_space=pl.ANY)
    vmem = pl.BlockSpec(memory_space=pltpu.VMEM)
    smem = pl.BlockSpec(memory_space=pltpu.SMEM)
    dma = pltpu.SemaphoreType.DMA
    regular = pltpu.SemaphoreType.REGULAR
    i32 = jnp.int32
    block = (FIELDS, BLOCKS, EXT, LANES)
    points, states = pl.pallas_call(
        whole,
        out_shape=(
            jax.ShapeDtypeStruct((1, FIELDS, ROWS, COLS), f32),
            jax.ShapeDtypeStruct((1, STEPS, ACT), f32),
        ),
        in_specs=[anywhere] * 4 + [smem] + [anywhere] * 3 + [smem],
        out_specs=(vmem, vmem),
        scratch_shapes=[
            pltpu.VMEM((STEPS + 1,) + block, f32),
            pltpu.VMEM((STEPS + 1,) + block, f32),
            pltpu.VMEM((STEPS,) + block, f32),
            pltpu.VMEM(block[1:], f32),
            pltpu.VMEM((STEPS, FIELDS, ROWS, COLS), bf16),
            pltpu.VMEM((2, FIELDS, BLOCKS, 8, LANES), f32),
            pltpu.VMEM((2, FIELDS, BLOCKS, 8, LANES), f32),
            pltpu.VMEM((ns, LANES), i32),
            pltpu.VMEM((ns, LANES), i32),
            pltpu.VMEM((ns, LANES), f32),
            pltpu.VMEM((FIELDS, BLOCKS, ROWS, LANES), jnp.int16),
            pltpu.VMEM((PIECES, 8, LANES), f32),
            pltpu.VMEM((FIELDS, BLOCKS, ROWS, LANES), jnp.int16),
            pltpu.VMEM((PIECES, 8, LANES), f32),
            pltpu.VMEM((ns // 2, COLS, 2 * LANES), bf16),
            pltpu.VMEM((ns // 2, ROWS, 2 * LANES), f32),
            pltpu.VMEM((2 * SETS * ROWS, COLS), bf16),
            pltpu.VMEM((SETS, ns, LANES), f32),
            pltpu.VMEM((ns, 1, LANES), f32),
            pltpu.VMEM((ns, 1, LANES), f32),
            pltpu.VMEM((nt, 1, LANES), f32),
            pltpu.VMEM((nt, 1, LANES), f32),
            pltpu.VMEM((1, LANES), f32),
            dma((16,)), dma((2,)), dma((2,)), dma((8,)), dma((8,)),
            dma((ns,)), dma((ns,)), dma((nt,)), dma((nt,)),
            regular, regular, regular,
        ],
        compiler_params=pltpu.CompilerParams(
            collective_id=0, has_side_effects=True, vmem_limit_bytes=58 * 2**20
        ),
        name="whole",
    )(c_points, terminal, forcing, conductance, coupling, flap_cells, flap_actuator, flap_area, actuator_rate)
    return (points, states)


def solution(mesh):
    placed = (
        P("tm", None, "space", None),
        P(None, "space", None),
        P("tm", None, None, "space", None),
        P("space", None),
        P(),
        P("space", None),
        P("space", None),
        P("space", None),
        P("space"),
    )
    return jax.shard_map(
        per_device,
        mesh=mesh,
        in_specs=placed,
        out_specs=(P("tm", None, "space", None), P("tm", None, "space")),
        check_vma=False,
    )
```

time: 216 us -> 45.1 us (0.21)
  the two profiles are of different devices: /device:TPU:8 before, /device:TPU:1 now
where the time goes in v3:
time: 45.1 us; the launch traced here: 44.9 us
  Pallas kernels  41.7 us (92%)
  local copies, waits for them, and re-layouts  2.57 us (6%)
  between operations  0.65 us (1%)
    pallas_call x1, Pallas kernels, per_device(): pl.pallas_call(whole, out_shape=(jax.ShapeDtypeStruct((1, FIELDS, ROWS, C...  41.7 us
    unnamed x4, local copies, waits for them, and re-layouts  2.57 us

profile of v3, /device:TPU:1, one launch (start us, length us, event | category | flops | bytes accessed | tf_op | source)
XLA Modules:
  0.0 44.9 jit_solution(3311078091090037531)
XLA Ops:
  0.6 41.7 %whole.1 = (f32[1,5,64,512]{3,2,1,0:T(8,128)}, f32[1,4,4]{2,1,0:T(4,128)}) custom-call(f32[1,5,64,512]{3,2,1,0:T(8,128)} %points_in.1, f32[5,64,512]{2,1,0:T(8,128)} %terminal.1, bf16[1,4,5,64,512]{4,3,2,1,0:T(8,128)(2,1)} %forcing.1, f32[64,512]{1,0:T(8,128)} %conductance.1, f32[5,5]{1,0:T(8,128)} %coupling_ref.1, s32[32,128]{1,0:T(8,128)} %cells_in.1, ...), custom_call_target="tpu_custom_call" | custom-call | tf_op jit(solution)/shard_map/whole/pallas_call | solution.py:495
  42.3 0.0 copy-start
  42.3 2.0 %copy.13 = f32[1,5,64,512]{3,2,1,0:T(8,128)} copy(f32[1,5,64,512]{3,2,1,0:T(8,128)} %get-tuple-element.4) | data formatting | bytes 1310720
  44.3 0.0 copy-done
  44.3 0.6 %copy.14 = f32[1,4,4]{2,1,0:T(4,128)} copy(f32[1,4,4]{2,1,0:T(4,128)S(1)} %copy-done) | data formatting | bytes 128
Async XLA Ops:
  42.3 2.0 %copy-start = (f32[1,4,4]{2,1,0:T(4,128)S(1)}, f32[1,4,4]{2,1,0:T(4,128)}, u32[]{:S(2)}) copy-start(f32[1,4,4]{2,1,0:T(4,128)} %get-tuple-element.5) | copy-start | bytes 196

commit v4 on v3

--- a/solution.py
+++ b/solution.py
@@ -18,6 +18,8 @@
 PIECES = ROWS // PIECE
 GROUP = STEPS * ACT
 SETS = 2 * STEPS
+RIM = 4
+INNER = ROWS - 2 * RIM
 MESH = pl.DeviceIdType.MESH
 LEVELS = 32767.0
 f32 = jnp.float32
@@ -30,34 +32,31 @@
 
 def step_map(src, cond, rows, coupling, lane):
     first, last = lane == 0, lane == LANES - 1
-    weight = [
-        jnp.concatenate([cond[b, pl.ds(row, 8), :] for row in rows], axis=0) for b in range(BLOCKS)
-    ]
     none = jnp.zeros(lane.shape, bf16)
-    mixed = []
+    left, right = {}, {}
     for f in range(FIELDS):
-        mid = [pair(src, f, b, rows, 0) for b in range(BLOCKS)]
-        short = [v.astype(bf16) for v in mid]
-        left = [pltpu.roll(v, 1, 1) for v in short]
-        right = [pltpu.roll(v, LANES - 1, 1) for v in short]
-        out = []
         for b in range(BLOCKS):
-            west = jnp.where(first, left[b - 1] if b else none, left[b])
-            east = jnp.where(last, right[b + 1] if b < BLOCKS - 1 else none, right[b])
-            flat = (jnp.bfloat16(3.0) * west + jnp.bfloat16(2.0) * east).astype(f32)
-            north, south = pair(src, f, b, rows, -1), pair(src, f, b, rows, 1)
-            beside = 0.35 * north + 0.15 * south + 0.1 * flat
-            out.append(mid[b] + weight[b] * (beside - mid[b]))
-        mixed.append(out)
-    result = []
-    for f in range(FIELDS):
-        row_out = []
-        for b in range(BLOCKS):
-            total = coupling[0][f] * mixed[0][b]
+            short = pair(src, f, b, rows, 0).astype(bf16)
+            left[f, b] = pltpu.roll(short, 1, 1)
+            right[f, b] = pltpu.roll(short, LANES - 1, 1)
+    result = [[None] * BLOCKS for _ in range(FIELDS)]
+    for b in range(BLOCKS):
+        weight = jnp.concatenate([cond[b, pl.ds(row, 8), :] for row in rows], axis=0)
+        keep, from_north, from_south, from_side = 1.0 - weight, 0.35 * weight, 0.15 * weight, 0.1 * weight
+        mixed = []
+        for f in range(FIELDS):
+            west = jnp.where(first, left[f, b - 1] if b else none, left[f, b])
+            east = jnp.where(last, right[f, b + 1] if b < BLOCKS - 1 else none, right[f, b])
+            side = (jnp.bfloat16(3.0) * west + jnp.bfloat16(2.0) * east).astype(f32)
+            mixed.append(
+                keep * pair(src, f, b, rows, 0) + from_north * pair(src, f, b, rows, -1)
+                + from_south * pair(src, f, b, rows, 1) + from_side * side
+            )
+        for f in range(FIELDS):
+            total = coupling[0][f] * mixed[0]
             for g in range(1, FIELDS):
-                total = total + coupling[g][f] * mixed[g][b]
-            row_out.append(total)
-        result.append(row_out)
+                total = total + coupling[g][f] * mixed[g]
+            result[f][b] = total
     return result
 
 
@@ -84,7 +83,7 @@
     points, states,
     free, forced, push, cond, force_own, force_out, force_in, cells, acts, area,
     coded, coded_scale, got, got_scale,
-    column, row_area, energy, picked, partial, mine, later, later_weight, send,
+    column, row_inner, row_rim, inner, rim, picked, picked_rim, partial, mine, later, later_weight, send, result_rows,
     in_sem, z_send, z_recv, s_send, s_recv, a_send, a_recv, t_send, t_recv,
     greet_y, greet_far, greet_farther,
 ):
@@ -128,7 +127,7 @@
     force_load = load(forcing.at[0], force_own, 8)
     slot_loads = [load(cells_in, cells, 9), load(acts_in, acts, 10), load(area_in, area, 11)]
     end_loads = columns(terminal, forced.at[0], 12)
-    for copy in first_loads + [force_load] + slot_loads:
+    for copy in slot_loads + [force_load] + first_loads[BLOCKS:] + first_loads[:BLOCKS]:
         copy.start()
 
     @pl.when(is_last)
@@ -161,21 +160,44 @@
                         part = part + add[f, b, pl.ds(row, 8), :]
                     dst[f, b, pl.ds(row, 8), :] = part
 
-    def interior(src, add, dst, j):
+    def interior(src, add, dst, j, beside=None):
         def body(i, carry):
-            row = jnp.minimum(EDGE + j + 16 * i, EDGE + ROWS - j - 16)
-            advance(src, add, dst, (row, row + 8))
+            for tile in (2 * i, 2 * i + 1):
+                if beside is not None:
+                    beside(tile)
+                row = jnp.minimum(EDGE + j + 16 * tile, EDGE + ROWS - j - 16)
+                advance(src, add, dst, (row, row + 8))
             return carry
 
-        lax.fori_loop(0, ROWS // 16, body, 0)
+        lax.fori_loop(0, ROWS // 32, body, 0)
 
     def edges(src, add, dst, j):
         advance(src, add, dst, (EDGE - 4 + j, EDGE + ROWS - 4 - j))
 
-    for copy in first_loads:
+    for copy in slot_loads:
         copy.wait()
-    interior(free.at[0], None, free.at[1], 1)
-    interior(free.at[1], None, free.at[2], 2)
+
+    numbers = lax.broadcasted_iota(jnp.int32, (COLS, LANES), 0).astype(jnp.int16)
+    one, zero = jnp.ones((16, LANES), bf16), jnp.zeros((16, LANES), bf16)
+
+    def slots(p, carry):
+        for half in range(2):
+            cell = cells[pl.ds(2 * p + half, 1), :]
+            lanes = pl.ds(half * LANES, LANES)
+            col = jnp.broadcast_to(jnp.bitwise_and(cell, COLS - 1), (16, LANES)).astype(jnp.int16)
+            for at in range(0, COLS, 16):
+                column[p, pl.ds(at, 16), lanes] = jnp.where(col == numbers[at : at + 16], one, zero)
+            row = jnp.broadcast_to(lax.shift_right_arithmetic(cell, 9), (INNER, LANES))
+            weight = jnp.broadcast_to(area[pl.ds(2 * p + half, 1), :], (INNER, LANES))
+            at = lax.broadcasted_iota(jnp.int32, (INNER, LANES), 0) + RIM
+            row_inner[p, :, lanes] = jnp.where(row == at, weight, 0.0)
+            at = lax.broadcasted_iota(jnp.int32, (2 * RIM, LANES), 0)
+            at = jnp.where(at < RIM, at, at + INNER)
+            row_rim[p, :, lanes] = jnp.where(row[: 2 * RIM] == at, weight[: 2 * RIM], 0.0)
+        return carry
+
+    lax.fori_loop(0, ns // 2, slots, 0)
+
 
     force_load.wait()
     for side, at in ((0, 13), (1, 0)):
@@ -203,11 +225,36 @@
         cond[:, high, :] = jnp.zeros((BLOCKS, 8, LANES), f32)
         force_in[1] = jnp.zeros((FIELDS, BLOCKS, 8, LANES), f32)
 
+    def widen(i, carry):
+        k, f = i // FIELDS, lax.rem(i, FIELDS)
+        value = force_own[k, f].astype(f32)
+        for b in range(BLOCKS):
+            push[k, f, b, own, :] = value[:, b * LANES : (b + 1) * LANES]
+        return carry
+
+    lax.fori_loop(0, STEPS * FIELDS, widen, 0)
+
+    for copy in first_loads[BLOCKS:]:
+        copy.wait()
+
     @pl.when(is_last)
     def _():
         for copy in end_loads:
             copy.wait()
 
+    @pl.when(has_later)
+    def _():
+        forced[1, :, :, own, :] = push[3, :, :, own, :]
+
+    @pl.when(is_last)
+    def _():
+        interior(forced.at[0], push.at[3], forced.at[1], 1)
+
+    for j in range(2, STEPS):
+        interior(forced.at[j - 1], push.at[STEPS - j], forced.at[j], j)
+
+    for copy in first_loads[:BLOCKS]:
+        copy.wait()
     pl.semaphore_wait(barrier, len(near_time) + 2 + len(near_space))
 
     def s_copy(src, dst, i, to):
@@ -246,51 +293,52 @@
     for j in far:
         signal(greet_far, in_time(j))
 
-    interior(free.at[2], None, free.at[3], 3)
-    interior(free.at[3], None, free.at[4], 4)
-
-    def widen(i, carry):
-        k, f = i // FIELDS, lax.rem(i, FIELDS)
-        value = force_own[k, f].astype(f32)
-        for b in range(BLOCKS):
-            push[k, f, b, own, :] = value[:, b * LANES : (b + 1) * LANES]
-        return carry
-
-    lax.fori_loop(0, STEPS * FIELDS, widen, 0)
-
-    @pl.when(has_later)
-    def _():
-        forced[1, :, :, own, :] = push[3, :, :, own, :]
-
-    @pl.when(is_last)
-    def _():
-        interior(forced.at[0], push.at[3], forced.at[1], 1)
+    parts = (forced, free)
+
+    def two_terms(value):
+        high = value.astype(bf16).astype(f32)
+        return jnp.concatenate([high, value - high], axis=0).astype(bf16)
+
+    def fill_inner(part):
+        for k in range(STEPS):
+            value = jnp.concatenate(
+                [parts[part][STEPS - k, 4, b, pl.ds(EDGE + RIM, INNER), :] for b in range(BLOCKS)], axis=1
+            )
+            inner[pl.ds(2 * INNER * (part * STEPS + k), 2 * INNER), :] = two_terms(value)
+
+    def pick(p, terms, first, sets, rows, weight, to):
+        out = jnp.dot(
+            terms[pl.ds(2 * rows * first, 2 * rows * sets), :], column[p], preferred_element_type=f32
+        )
+        for k in range(sets):
+            at = 2 * k * rows
+            both = (out[at : at + rows] + out[at + rows : at + 2 * rows]) * weight[p]
+            line = jnp.sum(both, axis=0, keepdims=True)
+            for half in range(2):
+                to[first + k, pl.ds(2 * p + half, 1), :] = line[:, half * LANES : (half + 1) * LANES]
+
+    def pick_inner(part, p):
+        pick(p, inner, part * STEPS, STEPS, INNER, row_inner, picked)
+
+    interior(forced.at[STEPS - 1], push.at[0], forced.at[STEPS], STEPS)
+    fill_inner(0)
+    pairs = ns // 2
+    tiles = ROWS // 16
+    shared = pairs >= STEPS * tiles
+    for j in range(1, STEPS + 1):
+        def some(i, j=j):
+            if shared:
+                pick_inner(0, (j - 1) * tiles + i)
+
+        interior(free.at[j - 1], None, free.at[j], j, some)
+    for p in range(STEPS * tiles if shared else 0, pairs):
+        pick_inner(0, p)
+    fill_inner(1)
 
     pl.semaphore_wait(greet_far, len(far))
     farther = offsets((4, -4), nt)
     for j in farther:
         signal(greet_farther, in_time(j))
-
-    for j in range(2, STEPS + 1):
-        interior(forced.at[j - 1], push.at[STEPS - j], forced.at[j], j)
-
-    for copy in slot_loads:
-        copy.wait()
-
-    def slots(p, carry):
-        for half in range(2):
-            cell = cells[pl.ds(2 * p + half, 1), :]
-            lanes = pl.ds(half * LANES, LANES)
-            col = jnp.broadcast_to(jnp.bitwise_and(cell, COLS - 1), (COLS, LANES))
-            at = lax.broadcasted_iota(jnp.int32, (COLS, LANES), 0)
-            column[p, :, lanes] = jnp.where(col == at, 1.0, 0.0).astype(bf16)
-            row = jnp.broadcast_to(lax.shift_right_arithmetic(cell, 9), (ROWS, LANES))
-            weight = jnp.broadcast_to(area[pl.ds(2 * p + half, 1), :], (ROWS, LANES))
-            at = lax.broadcasted_iota(jnp.int32, (ROWS, LANES), 0)
-            row_area[p, :, lanes] = jnp.where(row == at, weight, 0.0)
-        return carry
-
-    lax.fori_loop(0, ns // 2, slots, 0)
 
     for has, copies in ((has_down, up), (has_up, down)):
         @pl.when(has)
@@ -307,7 +355,15 @@
             row = EDGE - count if side == 0 else EDGE + ROWS
             push[k, :, :, pl.ds(row, count), :] = force_in[side, :, :, pl.ds(at, count), :]
 
+    todo = [0]
+
+    def some_free():
+        todo[0] += 1
+        for p in range((todo[0] - 1) * pairs // 7, todo[0] * pairs // 7):
+            pick_inner(1, p)
+
     for j in range(1, STEPS + 1):
+        some_free()
         edges(free.at[j - 1], None, free.at[j], j)
 
     for piece in range(PIECES):
@@ -345,33 +401,33 @@
         edges(forced.at[0], push.at[3], forced.at[1], 1)
 
     for j in range(2, STEPS + 1):
+        some_free()
         edges(forced.at[j - 1], push.at[STEPS - j], forced.at[j], j)
 
-    for part, ref in enumerate((forced, free)):
+    for part, ref in enumerate(parts):
         for k in range(STEPS):
-            value = jnp.concatenate([ref[STEPS - k, 4, b, own, :] for b in range(BLOCKS)], axis=1)
-            high = value.astype(bf16)
-            at = 2 * (part * STEPS + k) * ROWS
-            energy[pl.ds(at, ROWS), :] = high
-            energy[pl.ds(at + ROWS, ROWS), :] = (value - high.astype(f32)).astype(bf16)
-
-    def pick(p, carry):
-        out = jnp.dot(energy[...], column[p], preferred_element_type=f32)
-        weight = row_area[p]
-        for k in range(SETS):
-            at = 2 * k * ROWS
-            both = (out[at : at + ROWS] + out[at + ROWS : at + 2 * ROWS]) * weight
-            line = jnp.sum(both, axis=0, keepdims=True)
-            for half in range(2):
-                picked[k, pl.ds(2 * p + half, 1), :] = line[:, half * LANES : (half + 1) * LANES]
+            value = jnp.concatenate(
+                [
+                    jnp.concatenate(
+                        [ref[STEPS - k, 4, b, pl.ds(EDGE, RIM), :],
+                         ref[STEPS - k, 4, b, pl.ds(EDGE + ROWS - RIM, RIM), :]], axis=0
+                    )
+                    for b in range(BLOCKS)
+                ],
+                axis=1,
+            )
+            rim[pl.ds(4 * RIM * (part * STEPS + k), 4 * RIM), :] = two_terms(value)
+
+    def pick_rim(p, carry):
+        pick(p, rim, 0, SETS, 2 * RIM, row_rim, picked_rim)
         return carry
 
-    lax.fori_loop(0, ns // 2, pick, 0, unroll=4 if ns >= 8 else 1)
+    lax.fori_loop(0, pairs, pick_rim, 0, unroll=8 if pairs >= 8 else 1)
     ids = acts[...]
     wide = jnp.bitwise_and(lax.broadcasted_iota(jnp.int32, ids.shape, 1), 2 * GROUP - 1)
     total = jnp.zeros(ids.shape, f32)
     for k in range(SETS):
-        values = picked[k]
+        values = picked[k] + picked_rim[k]
         for a in range(ACT):
             part = jnp.sum(jnp.where(ids == a, values, 0.0), axis=1, keepdims=True)
             total = jnp.where(wide == k * ACT + a, part, total)
@@ -444,10 +500,12 @@
             factor = got_scale[piece, f : f + 1, :]
             for b in range(BLOCKS):
                 value = got[f, b, rows, :].astype(jnp.int32).astype(f32) * factor
-                points[0, f, rows, pl.ds(b * LANES, LANES)] = (
+                result_rows[f, rows, pl.ds(b * LANES, LANES)] = (
                     value + forced[STEPS, f, b, pl.ds(EDGE + piece * PIECE, PIECE), :]
                 )
 
+    store = load(result_rows, points.at[0], 8)
+    store.start()
     for j, copy in to_earlier.items():
         pl.when(t + j < nt)(copy.wait_recv)
     arrived = jnp.sum(later[...] * later_weight[...], axis=0)
@@ -461,6 +519,7 @@
         moved = pltpu.roll(result, LANES - ACT * k, 1) if k else result
         states[0, pl.ds(k, 1), :] = moved[:, :ACT]
 
+    store.wait()
     for j, copy in to_earlier.items():
         pl.when(t >= j)(copy.wait_send)
     for copy in to_owner:
@@ -479,6 +538,22 @@
     def _():
         for copy in z_copies:
             copy.wait_send()
+
+
+def hand_over(points_in, states_in, points, states, rows, small, sem):
+    into = [
+        pltpu.make_async_copy(points_in.at[0, f], rows.at[f], sem.at[0, f]) for f in range(FIELDS)
+    ] + [pltpu.make_async_copy(states_in, small, sem.at[0, FIELDS])]
+    out = [
+        pltpu.make_async_copy(rows.at[f], points.at[0, f], sem.at[1, f]) for f in range(FIELDS)
+    ] + [pltpu.make_async_copy(small, states, sem.at[1, FIELDS])]
+    for copy in into:
+        copy.start()
+    for first, then in zip(into, out):
+        first.wait()
+        then.start()
+    for copy in out:
+        copy.wait()
 
 
 def per_device(
@@ -499,7 +574,7 @@
             jax.ShapeDtypeStruct((1, STEPS, ACT), f32),
         ),
         in_specs=[anywhere] * 4 + [smem] + [anywhere] * 3 + [smem],
-        out_specs=(vmem, vmem),
+        out_specs=(anywhere, vmem),
         scratch_shapes=[
             pltpu.VMEM((STEPS + 1,) + block, f32),
             pltpu.VMEM((STEPS + 1,) + block, f32),
@@ -516,14 +591,18 @@
             pltpu.VMEM((FIELDS, BLOCKS, ROWS, LANES), jnp.int16),
             pltpu.VMEM((PIECES, 8, LANES), f32),
             pltpu.VMEM((ns // 2, COLS, 2 * LANES), bf16),
-            pltpu.VMEM((ns // 2, ROWS, 2 * LANES), f32),
-            pltpu.VMEM((2 * SETS * ROWS, COLS), bf16),
+            pltpu.VMEM((ns // 2, INNER, 2 * LANES), f32),
+            pltpu.VMEM((ns // 2, 2 * RIM, 2 * LANES), f32),
+            pltpu.VMEM((2 * SETS * INNER, COLS), bf16),
+            pltpu.VMEM((4 * SETS * RIM, COLS), bf16),
+            pltpu.VMEM((SETS, ns, LANES), f32),
             pltpu.VMEM((SETS, ns, LANES), f32),
             pltpu.VMEM((ns, 1, LANES), f32),
             pltpu.VMEM((ns, 1, LANES), f32),
             pltpu.VMEM((nt, 1, LANES), f32),
             pltpu.VMEM((nt, 1, LANES), f32),
             pltpu.VMEM((1, LANES), f32),
+            pltpu.VMEM((FIELDS, ROWS, COLS), f32),
             dma((16,)), dma((2,)), dma((2,)), dma((8,)), dma((8,)),
             dma((ns,)), dma((ns,)), dma((nt,)), dma((nt,)),
             regular, regular, regular,
@@ -533,7 +612,20 @@
         ),
         name="whole",
     )(c_points, terminal, forcing, conductance, coupling, flap_cells, flap_actuator, flap_area, actuator_rate)
-    return (points, states)
+    return pl.pallas_call(
+        hand_over,
+        out_shape=(
+            jax.ShapeDtypeStruct(points.shape, f32),
+            jax.ShapeDtypeStruct(states.shape, f32),
+        ),
+        in_specs=[anywhere] * 2,
+        out_specs=(anywhere,) * 2,
+        scratch_shapes=[
+            pltpu.VMEM((FIELDS, ROWS, COLS), f32), pltpu.VMEM(states.shape, f32), dma((2, FIELDS + 1))
+        ],
+        compiler_params=pltpu.CompilerParams(vmem_limit_bytes=60 * 2**20),
+        name="hand_over",
+    )(points, states)
 
 
 def solution(mesh):

time: 45.1 us -> 41.3 us (0.916)
  local copies, waits for them, and re-layouts: 2.57 us -> 0 us
  Pallas kernels: 41.7 us -> 40.4 us
    pallas_call x1, Pallas kernels: 41.7 us -> 38.5 us  [per_device(): pl.pallas_call(whole, out_shape=(jax.ShapeDtypeStruct((1, FIELDS, ROWS, C...]
    unnamed x4 -> x0, local copies, waits for them, and re-layouts: 2.57 us -> none
    pallas_call x0 -> x1, Pallas kernels: none -> 1.93 us  [per_device(): pl.pallas_call(hand_over, out_shape=(jax.ShapeDtypeStruct(points.shape, f...]
where the time goes in v4:
time: 41.3 us; the launch traced here: 41.1 us
  Pallas kernels  40.4 us (98%)
  between operations  0.64 us (2%)
    pallas_call x1, Pallas kernels, per_device(): pl.pallas_call(whole, out_shape=(jax.ShapeDtypeStruct((1, FIELDS, ROWS, C...  38.5 us
    pallas_call x1, Pallas kernels, per_device(): pl.pallas_call(hand_over, out_shape=(jax.ShapeDtypeStruct(points.shape, f...  1.93 us

profile of v4, /device:TPU:1, one launch (start us, length us, event | category | flops | bytes accessed | tf_op | source)
XLA Modules:
  0.0 41.1 jit_solution(5614882992869744996)
XLA Ops:
  0.6 38.5 %whole.1 = (f32[1,5,64,512]{3,2,1,0:T(8,128)}, f32[1,4,4]{2,1,0:T(4,128)}) custom-call(f32[1,5,64,512]{3,2,1,0:T(8,128)} %points_in.1, f32[5,64,512]{2,1,0:T(8,128)} %terminal.1, bf16[1,4,5,64,512]{4,3,2,1,0:T(8,128)(2,1)} %forcing.1, f32[64,512]{1,0:T(8,128)} %conductance.1, f32[5,5]{1,0:T(8,128)} %coupling_ref.1, s32[32,128]{1,0:T(8,128)} %cells_in.1, ...), custom_call_target="tpu_custom_call" | custom-call | tf_op jit(solution)/shard_map/whole/pallas_call | solution.py:570
  39.2 1.9 %hand_over.1 = (f32[1,5,64,512]{3,2,1,0:T(8,128)}, f32[1,4,4]{2,1,0:T(4,128)}) custom-call(f32[1,5,64,512]{3,2,1,0:T(8,128)} %get-tuple-element.4.points_in, f32[1,4,4]{2,1,0:T(4,128)} %get-tuple-element.5.states_in), custom_call_target="tpu_custom_call" | custom-call | tf_op jit(solution)/shard_map/hand_over/pallas_call | solution.py:615

commit v5 on v4

--- a/solution.py
+++ b/solution.py
@@ -81,7 +81,8 @@
 def whole(
     points_in, terminal, forcing, conductance, coupling_ref, cells_in, acts_in, area_in, rate_ref,
     points, states,
-    free, forced, push, cond, force_own, force_out, force_in, cells, acts, area,
+    free, forced, push, cond, force_own, force_rows, force_out, force_in,
+    start_out, start_in, end_out, end_in, cells, acts, area,
     coded, coded_scale, got, got_scale,
     column, row_inner, row_rim, inner, rim, picked, picked_rim, partial, mine, later, later_weight, send, result_rows,
     in_sem, z_send, z_recv, s_send, s_recv, a_send, a_recv, t_send, t_recv,
@@ -161,15 +162,17 @@
                     dst[f, b, pl.ds(row, 8), :] = part
 
     def interior(src, add, dst, j, beside=None):
+        per = 2 if beside is None else 4
+
         def body(i, carry):
-            for tile in (2 * i, 2 * i + 1):
+            for tile in [per * i + n for n in range(per)]:
                 if beside is not None:
                     beside(tile)
                 row = jnp.minimum(EDGE + j + 16 * tile, EDGE + ROWS - j - 16)
                 advance(src, add, dst, (row, row + 8))
             return carry
 
-        lax.fori_loop(0, ROWS // 32, body, 0)
+        lax.fori_loop(0, ROWS // 16 // per, body, 0)
 
     def edges(src, add, dst, j):
         advance(src, add, dst, (EDGE - 4 + j, EDGE + ROWS - 4 - j))
@@ -200,31 +203,6 @@
 
 
     force_load.wait()
-    for side, at in ((0, 13), (1, 0)):
-        for f in range(FIELDS):
-            for k, count, to in ((3, 3, 0), (2, 2, 3), (1, 1, 5)):
-                near = force_own[k, f, pl.ds(ROWS - 16 if side == 0 else 0, 16), :].astype(f32)
-                near = near[16 - count :] if side == 0 else near[:count]
-                for b in range(BLOCKS):
-                    force_out[side, f, b, pl.ds(to, count), :] = near[:, b * LANES : (b + 1) * LANES]
-            for b in range(BLOCKS):
-                force_out[side, f, b, pl.ds(6, 2), :] = jnp.zeros((2, LANES), f32)
-
-    @pl.when(jnp.logical_not(has_down))
-    def _():
-        free[0, :, :, pl.ds(8, 8), :] = jnp.zeros((FIELDS, BLOCKS, 8, LANES), f32)
-        forced[0, :, :, pl.ds(8, 8), :] = jnp.zeros((FIELDS, BLOCKS, 8, LANES), f32)
-        cond[:, pl.ds(8, 8), :] = jnp.zeros((BLOCKS, 8, LANES), f32)
-        force_in[0] = jnp.zeros((FIELDS, BLOCKS, 8, LANES), f32)
-
-    @pl.when(jnp.logical_not(has_up))
-    def _():
-        high = pl.ds(EDGE + ROWS, 8)
-        free[0, :, :, high, :] = jnp.zeros((FIELDS, BLOCKS, 8, LANES), f32)
-        forced[0, :, :, high, :] = jnp.zeros((FIELDS, BLOCKS, 8, LANES), f32)
-        cond[:, high, :] = jnp.zeros((BLOCKS, 8, LANES), f32)
-        force_in[1] = jnp.zeros((FIELDS, BLOCKS, 8, LANES), f32)
-
     def widen(i, carry):
         k, f = i // FIELDS, lax.rem(i, FIELDS)
         value = force_own[k, f].astype(f32)
@@ -234,6 +212,40 @@
 
     lax.fori_loop(0, STEPS * FIELDS, widen, 0)
 
+    needs = ((3, 3, 0), (2, 2, 3), (1, 1, 5))
+    near = (EDGE + ROWS, EDGE)
+    for side in range(2):
+        for b in range(BLOCKS):
+            for f in range(FIELDS):
+                for k, count, at in needs:
+                    row = near[side] - count if side == 0 else near[side]
+                    force_rows[side, b, pl.ds(6 * f + at, count), :] = push[k, f, b, pl.ds(row, count), :]
+            force_rows[side, b, pl.ds(6 * FIELDS, 2), :] = jnp.zeros((2, LANES), f32)
+            force_out[side, b] = force_rows[side, b].astype(bf16)
+
+    def pack(ref, out):
+        for side in range(2):
+            row = near[side] - 4 if side == 0 else near[side]
+            for b in range(BLOCKS):
+                for f in range(FIELDS):
+                    out[side, b, pl.ds(4 * f, 4), :] = ref[f, b, pl.ds(row, 4), :]
+                out[side, b, pl.ds(4 * FIELDS, 4), :] = jnp.zeros((4, LANES), f32)
+
+    def unpack(got_rows, ref):
+        for side in range(2):
+            row = EDGE - 4 if side == 0 else EDGE + ROWS
+            for b in range(BLOCKS):
+                for f in range(FIELDS):
+                    ref[f, b, pl.ds(row, 4), :] = got_rows[side, b, pl.ds(4 * f, 4), :]
+
+    for side, has, row in ((0, has_down, 8), (1, has_up, EDGE + ROWS)):
+        @pl.when(jnp.logical_not(has))
+        def _(side=side, row=row):
+            start_in[side] = jnp.zeros(start_in.shape[1:], f32)
+            end_in[side] = jnp.zeros(end_in.shape[1:], f32)
+            cond[:, pl.ds(row, 8), :] = jnp.zeros((BLOCKS, 8, LANES), f32)
+            force_in[side] = jnp.zeros(force_in.shape[1:], bf16)
+
     for copy in first_loads[BLOCKS:]:
         copy.wait()
 
@@ -248,50 +260,8 @@
 
     @pl.when(is_last)
     def _():
+        pack(forced.at[0], end_out)
         interior(forced.at[0], push.at[3], forced.at[1], 1)
-
-    for j in range(2, STEPS):
-        interior(forced.at[j - 1], push.at[STEPS - j], forced.at[j], j)
-
-    for copy in first_loads[:BLOCKS]:
-        copy.wait()
-    pl.semaphore_wait(barrier, len(near_time) + 2 + len(near_space))
-
-    def s_copy(src, dst, i, to):
-        return pltpu.make_async_remote_copy(
-            src_ref=src, dst_ref=dst, send_sem=s_send.at[i], recv_sem=s_recv.at[i],
-            device_id=(t, to), device_id_type=MESH,
-        )
-
-    def halo(side):
-        to = s + 1 if side == 0 else s - 1
-        mine_rows = pl.ds(EDGE + ROWS - 8 if side == 0 else EDGE, 8)
-        their_rows = pl.ds(8 if side == 0 else EDGE + ROWS, 8)
-        i = 4 * side
-        return [
-            s_copy(free.at[0, :, :, mine_rows, :], free.at[0, :, :, their_rows, :], i, to),
-            s_copy(cond.at[:, mine_rows, :], cond.at[:, their_rows, :], i + 1, to),
-            s_copy(force_out.at[side], force_in.at[side], i + 2, to),
-            s_copy(forced.at[0, :, :, mine_rows, :], forced.at[0, :, :, their_rows, :], i + 3, to),
-        ]
-
-    up, down = halo(0), halo(1)
-    for has, copies in ((has_up, up), (has_down, down)):
-        @pl.when(has)
-        def _(copies=copies):
-            for copy in copies[:3]:
-                copy.start()
-
-        @pl.when(jnp.logical_and(has, is_last))
-        def _(copies=copies):
-            copies[3].start()
-
-    same_x = [o for o in near_space if o[1:] == (0, 0)]
-    for o in same_x:
-        signal(greet_y, beside(o))
-    far = offsets((2, -2), nt)
-    for j in far:
-        signal(greet_far, in_time(j))
 
     parts = (forced, free)
 
@@ -299,12 +269,13 @@
         high = value.astype(bf16).astype(f32)
         return jnp.concatenate([high, value - high], axis=0).astype(bf16)
 
-    def fill_inner(part):
-        for k in range(STEPS):
+    def fill_inner(part, stages):
+        for stage in stages:
             value = jnp.concatenate(
-                [parts[part][STEPS - k, 4, b, pl.ds(EDGE + RIM, INNER), :] for b in range(BLOCKS)], axis=1
+                [parts[part][stage, 4, b, pl.ds(EDGE + RIM, INNER), :] for b in range(BLOCKS)], axis=1
             )
-            inner[pl.ds(2 * INNER * (part * STEPS + k), 2 * INNER), :] = two_terms(value)
+            at = 2 * INNER * (part * STEPS + STEPS - stage)
+            inner[pl.ds(at, 2 * INNER), :] = two_terms(value)
 
     def pick(p, terms, first, sets, rows, weight, to):
         out = jnp.dot(
@@ -317,23 +288,88 @@
             for half in range(2):
                 to[first + k, pl.ds(2 * p + half, 1), :] = line[:, half * LANES : (half + 1) * LANES]
 
-    def pick_inner(part, p):
-        pick(p, inner, part * STEPS, STEPS, INNER, row_inner, picked)
-
-    interior(forced.at[STEPS - 1], push.at[0], forced.at[STEPS], STEPS)
-    fill_inner(0)
+    def pick_inner(first, sets, p):
+        pick(p, inner, first, sets, INNER, row_inner, picked)
+
     pairs = ns // 2
+
+    def share(first, sets, turns):
+        count = -(-pairs // turns)
+
+        def turn(i):
+            for n in range(count):
+                if pairs == turns * count:
+                    pick_inner(first, sets, count * i + n)
+
+        return turn if pairs == turns * count else None
+
+    def rest(first, sets, turns):
+        if share(first, sets, turns) is None:
+            for p in range(pairs):
+                pick_inner(first, sets, p)
+
     tiles = ROWS // 16
-    shared = pairs >= STEPS * tiles
-    for j in range(1, STEPS + 1):
-        def some(i, j=j):
-            if shared:
-                pick_inner(0, (j - 1) * tiles + i)
-
-        interior(free.at[j - 1], None, free.at[j], j, some)
-    for p in range(STEPS * tiles if shared else 0, pairs):
-        pick_inner(0, p)
-    fill_inner(1)
+    fill_inner(0, (1,))
+    first_share = share(3, 1, 2 * tiles)
+    interior(forced.at[1], push.at[2], forced.at[2], 2, first_share)
+    for copy in first_loads[:BLOCKS]:
+        copy.wait()
+    pack(free.at[0], start_out)
+    pl.semaphore_wait(barrier, len(near_time) + 2 + len(near_space))
+
+    def s_copy(src, dst, i, to):
+        return pltpu.make_async_remote_copy(
+            src_ref=src, dst_ref=dst, send_sem=s_send.at[i], recv_sem=s_recv.at[i],
+            device_id=(t, to), device_id_type=MESH,
+        )
+
+    def halo(side):
+        to = s + 1 if side == 0 else s - 1
+        mine_rows = pl.ds(EDGE + ROWS - 8 if side == 0 else EDGE, 8)
+        their_rows = pl.ds(8 if side == 0 else EDGE + ROWS, 8)
+        i = 4 * side
+        return [
+            s_copy(start_out.at[side], start_in.at[side], i, to),
+            s_copy(cond.at[:, mine_rows, :], cond.at[:, their_rows, :], i + 1, to),
+            s_copy(force_out.at[side], force_in.at[side], i + 2, to),
+            s_copy(end_out.at[side], end_in.at[side], i + 3, to),
+        ]
+
+    up, down = halo(0), halo(1)
+    for has, copies in ((has_up, up), (has_down, down)):
+        @pl.when(has)
+        def _(copies=copies):
+            for copy in copies[:3]:
+                copy.start()
+
+        @pl.when(jnp.logical_and(has, is_last))
+        def _(copies=copies):
+            copies[3].start()
+
+    same_x = [o for o in near_space if o[1:] == (0, 0)]
+    for o in same_x:
+        signal(greet_y, beside(o))
+    far = offsets((2, -2), nt)
+    for j in far:
+        signal(greet_far, in_time(j))
+
+    def shifted(turn, by):
+        return None if turn is None else lambda i: turn(i + by)
+
+    interior(forced.at[2], push.at[1], forced.at[3], 3, shifted(first_share, tiles))
+    interior(forced.at[3], push.at[0], forced.at[4], 4)
+    rest(3, 1, 2 * tiles)
+    fill_inner(0, (2, 3, 4))
+    second_share = share(0, 3, 2 * tiles)
+    interior(free.at[0], None, free.at[1], 1, second_share)
+    interior(free.at[1], None, free.at[2], 2, shifted(second_share, tiles))
+    rest(0, 3, 2 * tiles)
+    fill_inner(1, (1, 2))
+    third_share = share(STEPS + 2, 2, 2 * tiles)
+    interior(free.at[2], None, free.at[3], 3, third_share)
+    interior(free.at[3], None, free.at[4], 4, shifted(third_share, tiles))
+    rest(STEPS + 2, 2, 2 * tiles)
+    fill_inner(1, (3, 4))
 
     pl.semaphore_wait(greet_far, len(far))
     farther = offsets((4, -4), nt)
@@ -350,17 +386,21 @@
         def _(copies=copies):
             copies[3].wait_recv()
 
+    unpack(start_in, free.at[0])
     for side in range(2):
-        for k, count, at in ((3, 3, 0), (2, 2, 3), (1, 1, 5)):
-            row = EDGE - count if side == 0 else EDGE + ROWS
-            push[k, :, :, pl.ds(row, count), :] = force_in[side, :, :, pl.ds(at, count), :]
+        for b in range(BLOCKS):
+            force_rows[side, b] = force_in[side, b].astype(f32)
+            for f in range(FIELDS):
+                for k, count, at in needs:
+                    row = EDGE - count if side == 0 else EDGE + ROWS
+                    push[k, f, b, pl.ds(row, count), :] = force_rows[side, b, pl.ds(6 * f + at, count), :]
 
     todo = [0]
 
     def some_free():
         todo[0] += 1
         for p in range((todo[0] - 1) * pairs // 7, todo[0] * pairs // 7):
-            pick_inner(1, p)
+            pick_inner(STEPS, 2, p)
 
     for j in range(1, STEPS + 1):
         some_free()
@@ -398,6 +438,7 @@
 
     @pl.when(is_last)
     def _():
+        unpack(end_in, forced.at[0])
         edges(forced.at[0], push.at[3], forced.at[1], 1)
 
     for j in range(2, STEPS + 1):
@@ -422,7 +463,7 @@
         pick(p, rim, 0, SETS, 2 * RIM, row_rim, picked_rim)
         return carry
 
-    lax.fori_loop(0, pairs, pick_rim, 0, unroll=8 if pairs >= 8 else 1)
+    lax.fori_loop(0, pairs, pick_rim, 0, unroll=pairs)
     ids = acts[...]
     wide = jnp.bitwise_and(lax.broadcasted_iota(jnp.int32, ids.shape, 1), 2 * GROUP - 1)
     total = jnp.zeros(ids.shape, f32)
@@ -581,8 +622,13 @@
             pltpu.VMEM((STEPS,) + block, f32),
             pltpu.VMEM(block[1:], f32),
             pltpu.VMEM((STEPS, FIELDS, ROWS, COLS), bf16),
-            pltpu.VMEM((2, FIELDS, BLOCKS, 8, LANES), f32),
-            pltpu.VMEM((2, FIELDS, BLOCKS, 8, LANES), f32),
+            pltpu.VMEM((2, BLOCKS, 32, LANES), f32),
+            pltpu.VMEM((2, BLOCKS, 32, LANES), bf16),
+            pltpu.VMEM((2, BLOCKS, 32, LANES), bf16),
+            pltpu.VMEM((2, BLOCKS, 24, LANES), f32),
+            pltpu.VMEM((2, BLOCKS, 24, LANES), f32),
+            pltpu.VMEM((2, BLOCKS, 24, LANES), f32),
+            pltpu.VMEM((2, BLOCKS, 24, LANES), f32),
             pltpu.VMEM((ns, LANES), i32),
             pltpu.VMEM((ns, LANES), i32),
             pltpu.VMEM((ns, LANES), f32),

time: 41.3 us -> 40.3 us (0.976)
  Pallas kernels: 40.4 us -> 39.4 us
    pallas_call x1, Pallas kernels: 38.5 us -> 37.5 us  [per_device(): pl.pallas_call(whole, out_shape=(jax.ShapeDtypeStruct((1, FIELDS, ROWS, C...]
where the time goes in v5:
time: 40.3 us; the launch traced here: 40 us
  Pallas kernels  39.4 us (98%)
  between operations  0.64 us (2%)
    pallas_call x1, Pallas kernels, per_device(): pl.pallas_call(whole, out_shape=(jax.ShapeDtypeStruct((1, FIELDS, ROWS, C...  37.5 us
    pallas_call x1, Pallas kernels, per_device(): pl.pallas_call(hand_over, out_shape=(jax.ShapeDtypeStruct(points.shape, f...  1.93 us

profile of v5, /device:TPU:1, one launch (start us, length us, event | category | flops | bytes accessed | tf_op | source)
XLA Modules:
  0.0 40.0 jit_solution(17962152198954833808)
XLA Ops:
  0.6 37.5 %whole.1 = (f32[1,5,64,512]{3,2,1,0:T(8,128)}, f32[1,4,4]{2,1,0:T(4,128)}) custom-call(f32[1,5,64,512]{3,2,1,0:T(8,128)} %points_in.1, f32[5,64,512]{2,1,0:T(8,128)} %terminal.1, bf16[1,4,5,64,512]{4,3,2,1,0:T(8,128)(2,1)} %forcing.1, f32[64,512]{1,0:T(8,128)} %conductance.1, f32[5,5]{1,0:T(8,128)} %coupling_ref.1, s32[32,128]{1,0:T(8,128)} %cells_in.1, ...), custom_call_target="tpu_custom_call" | custom-call | tf_op jit(solution)/shard_map/whole/pallas_call | solution.py:611
  38.1 1.9 %hand_over.1 = (f32[1,5,64,512]{3,2,1,0:T(8,128)}, f32[1,4,4]{2,1,0:T(4,128)}) custom-call(f32[1,5,64,512]{3,2,1,0:T(8,128)} %get-tuple-element.4.points_in, f32[1,4,4]{2,1,0:T(4,128)} %get-tuple-element.5.states_in), custom_call_target="tpu_custom_call" | custom-call | tf_op jit(solution)/shard_map/hand_over/pallas_call | solution.py:661
